TPU v7x, 128 devices: a whole 4x4x4 slice. The times are simulated.
128 devices in a mesh: row: 16 (over y_hi, z, core), col: 8 (over y_lo, x).
Axes of the slice: x: 4, y: 4 (y_hi: 2, y_lo: 2; y = y_hi * 2 + y_lo), z: 4, core: 2. Of those that a mesh axis runs over, the one named last changes fastest.
Arguments:
- pair_rep: bfloat16 [512, 512, 128], P('row', 'col'), may hold values from -6 to 6
- in_gain: float32 [128], replicated, may hold values from 0.25 to 1.75
- in_bias: float32 [128], replicated, may hold values from -3 to 3
- w_left_gate: bfloat16 [128, 128], replicated, may hold values from -0.5 to 0.5
- w_left: bfloat16 [128, 128], replicated, may hold values from -0.5 to 0.5
- w_right_gate: bfloat16 [128, 128], replicated, may hold values from -0.5 to 0.5
- w_right: bfloat16 [128, 128], replicated, may hold values from -0.5 to 0.5
- out_gain: float32 [128], replicated, may hold values from 0.25 to 1.75
- out_bias: float32 [128], replicated, may hold values from -3 to 3
- w_out_gate: bfloat16 [128, 128], replicated, may hold values from -0.5 to 0.5
- w_out: bfloat16 [128, 128], replicated, may hold values from -0.5 to 0.5
Outputs:
- update: float32 [512, 512, 128], P('row', 'col')
All inputs are finite; a program needn't handle non-finite values.
Results may differ from a plain program's by a relative error of at most 0.0037.
Values may be sent and summed in bfloat16 or wider, within the bound.
No kernel may reach another device: no remote copies, remote signals or barrier semaphores. Data moves between devices by JAX's collectives and lax.ppermute only.
A program may use at most 128 MiB of HBM per device.

v0:
```python
import jax
import jax.numpy as jnp
from jax import lax
from jax.sharding import PartitionSpec as P

EPS = 1e-05


def spread(value, axis, source):
    kept = jnp.where(lax.axis_index(axis) == source, value, 0).astype(value.dtype)
    return lax.psum(kept, axis)


def layer_norm(values, norm_gain, norm_bias, axis_pos):
    mean_val = jnp.mean(values, axis_pos, keepdims=True)
    variance = jnp.mean(jnp.square(values - mean_val), axis_pos, keepdims=True)
    return (values - mean_val) * lax.rsqrt(variance + EPS) * norm_gain + norm_bias


def gated_proj(normed, w_gate, w_proj):
    gate_val = jnp.einsum("ikd,dc->cik", normed, w_gate, preferred_element_type=jnp.float32)
    proj_val = jnp.einsum("ikd,dc->cik", normed, w_proj, preferred_element_type=jnp.float32)
    return (jax.nn.sigmoid(gate_val) * proj_val).astype(jnp.bfloat16)


def per_device(
    pair_rep,
    in_gain,
    in_bias,
    w_left_gate,
    w_left,
    w_right_gate,
    w_right,
    out_gain,
    out_bias,
    w_out_gate,
    w_out,
):
    normed = layer_norm(pair_rep.astype(jnp.float32), in_gain, in_bias, -1).astype(jnp.bfloat16)
    left_proj = gated_proj(normed, w_left_gate, w_left)
    stride_rows = lax.axis_size("row") // lax.axis_size("col")
    col_index = lax.axis_index("col")
    right_proj = gated_proj(normed, w_right_gate, w_right)
    left_all, right_all = (
        lax.all_gather(left_proj, "col", axis=2, tiled=True),
        lax.all_gather(right_proj, "col", axis=2, tiled=True),
    )
    blocks = [
        spread(right_all, "row", col_index * stride_rows + member) for member in range(stride_rows)
    ]
    right_cols = jnp.concatenate(blocks, 1)
    mixed_sum = jnp.einsum("cik,cjk->cij", left_all, right_cols, preferred_element_type=jnp.float32)
    mixed_norm = layer_norm(mixed_sum, out_gain[:, None, None], out_bias[:, None, None], 0).astype(
        jnp.bfloat16
    )
    gate_act = jax.nn.sigmoid(
        jnp.einsum("ijd,de->ije", normed, w_out_gate, preferred_element_type=jnp.float32)
    )
    projected = jnp.einsum("cij,cd->ijd", mixed_norm, w_out, preferred_element_type=jnp.float32)
    return gate_act * projected


def solution(mesh):
    placed = (P("row", "col", None), P(), P(), P(), P(), P(), P(), P(), P(), P(), P())
    return jax.shard_map(
        per_device, mesh=mesh, in_specs=placed, out_specs=P("row", "col", None), check_vma=False
    )
```

profile of v0, /device:TPU:1, one launch (start us, length us, event | category | flops | bytes accessed | tf_op | source)
XLA Modules:
  0.0 323.1 jit_solution(5523875019315098304)
XLA Ops:
  6.5 0.0 copy-start
  6.5 0.0 all-gather.5.cloned.1.call-start
  6.5 1.4 convert_reduce_fusion
  7.9 1.7 fusion.17
  9.6 0.0 copy-start.1
  9.6 0.0 copy-start.3
  9.7 0.0 copy-start.4
  9.7 0.0 copy-start.5
  9.7 0.0 copy-done
  9.7 1.8 fusion.23
  11.6 2.6 fusion.16
  14.2 0.0 all-gather.5.cloned.1.call-update
  14.2 0.0 all-gather.3.cloned.1.call-start
  14.3 0.7 fusion.26
  15.0 1.7 fusion.15
  16.7 0.0 all-gather.3.cloned.1.call-update
  16.7 0.0 all-reduce.3.cloned.1.call-start
  16.8 53.3 %all-gather.5.cloned.1.call-done = bf16[128,32,512]{0,2,1:T(8,128)(2,1)} async-done(((bf16[128,32,64]{0,2,1:T(8,128)(2,1)}), bf16[128,32,512]{0,2,1:T(8,128)(2,1)}) %all-gather.5.cloned.1.call-update) | async-done | bytes 4194320 | tf_op jit(solution)/shard_map/all_gather | solution.py:46
  70.1 6.1 %broadcast_select_fusion.1 = (bf16[128,32,512]{0,2,1:T(8,128)(2,1)}, bf16[128,32,512]{0,2,1:T(8,128)(2,1)}) fusion(bf16[128,32,512]{0,2,1:T(8,128)(2,1)} %all-gather.5.cloned.1.call-done, pred[]{:T(512)S(6)} %eq.6, pred[]{:T(512)S(6)} %eq.7), kind=kLoop, calls=%fused_computation.2 | loop fusion | flops 4194304 | bytes 12582914 | tf_op jit(solution)/shard_map/jit(_where)/select_n | solution.py:10
  76.2 0.0 all-reduce.3.cloned.1.call-update
  76.3 0.7 copy-done.9
  77.0 0.7 fusion.4
  77.7 45.4 %all-gather.3.cloned.1.call-done = bf16[128,32,512]{0,2,1:T(8,128)(2,1)} async-done(((bf16[128,32,64]{0,2,1:T(8,128)(2,1)}), bf16[128,32,512]{0,2,1:T(8,128)(2,1)}) %all-gather.3.cloned.1.call-update) | async-done | bytes 4194320 | tf_op jit(solution)/shard_map/all_gather | solution.py:45
  123.2 8.0 %copy.12 = bf16[128,32,512]{2,1,0:T(8,128)(2,1)} copy(bf16[128,32,512]{0,2,1:T(8,128)(2,1)} %all-gather.3.cloned.1.call-done) | data formatting | bytes 8388608 | tf_op jit(solution)/shard_map/all_gather | solution.py:45
  131.1 156.3 %all-reduce.3.cloned.1.call-done = (bf16[128,32,512]{0,2,1:T(8,128)(2,1)}, bf16[128,32,512]{0,2,1:T(8,128)(2,1)}) async-done(((bf16[128,32,512]{0,2,1:T(8,128)(2,1)}, bf16[128,32,512]{0,2,1:T(8,128)(2,1)}), (bf16[128,32,512]{0,2,1:T(8,128)(2,1)}, bf16[128,32,512]{0,2,1:T(8,128)(2,1)})) %all-reduce.3.cloned.1.call-update) | async-done | bytes 8388624 | tf_op jit(solution)/shard_map/psum | solution.py:11
  287.4 7.4 %pad_maximum_fusion = bf16[128,64,512]{0,2,1:T(8,128)(2,1)} fusion(bf16[128,32,512]{0,2,1:T(8,128)(2,1)} %get-tuple-element.5, bf16[128,32,512]{0,2,1:T(8,128)(2,1)} %get-tuple-element.6), kind=kLoop, calls=%fused_computation | loop fusion | flops 4194304 | bytes 16777216 | tf_op jit(solution)/shard_map/concatenate | solution.py:51
  294.9 12.4 %copy.13 = bf16[128,64,512]{2,1,0:T(8,128)(2,1)} copy(bf16[128,64,512]{0,2,1:T(8,128)(2,1)} %pad_maximum_fusion) | data formatting | bytes 16777216 | tf_op jit(solution)/shard_map/concatenate | solution.py:51
  307.3 7.0 %fusion.35 = (f32[32,64]{1,0:T(8,128)S(1)}, f32[128,32,64]{2,1,0:T(8,128)S(1)}) fusion(bf16[128,32,512]{2,1,0:T(8,128)(2,1)} %copy.12, bf16[128,64,512]{2,1,0:T(8,128)(2,1)} %copy.13), kind=kOutput, calls=%fused_computation.45 | convolution fusion | flops 268695552 | bytes 13639680 | tf_op jit(solution)/shard_map/cik,cjk->cij/dot_general | solution.py:52
  314.2 0.0 copy-start.2
  314.3 0.3 multiply_reduce_fusion
  314.6 0.4 add_convert_fusion
  315.1 1.5 convolution_multiply_fusion
  (16 shorter events, 0.1 us)
Async XLA Ops:
  6.5 3.2 copy-start
  6.5 63.6 %all-gather.5.cloned.1.call-start = ((), (), s32[]{:S(2)}) async-start(), calls=%async_computation.1 | async-start | bytes 4718592 | tf_op jit(solution)/shard_map/all_gather | solution.py:46
  9.6 4.6 %copy-start.1 = (bf16[32,64,128]{2,1,0:T(8,128)(2,1)S(1)}, bf16[32,64,128]{2,1,0:T(8,128)(2,1)}, u32[]{:S(2)}) copy-start(bf16[32,64,128]{2,1,0:T(8,128)(2,1)} %param.11) | copy-start | bytes 1572868
  9.6 4.6 %copy-start.3 = (bf16[128,128]{1,0:T(8,128)(2,1)S(1)}, bf16[128,128]{1,0:T(8,128)(2,1)}, u32[]{:S(2)}) copy-start(bf16[128,128]{1,0:T(8,128)(2,1)} %param.15) | copy-start | bytes 98308
  9.7 4.6 %copy-start.4 = (f32[128]{0:T(128)S(1)}, f32[128]{0:T(128)}, u32[]{:S(2)}) copy-start(f32[128]{0:T(128)} %param.13) | copy-start | bytes 1540
  9.7 4.6 %copy-start.5 = (f32[128]{0:T(128)S(1)}, f32[128]{0:T(128)}, u32[]{:S(2)}) copy-start(f32[128]{0:T(128)} %param.12) | copy-start | bytes 1540
  11.5 3.5 %copy-start.8 = (bf16[128,128]{1,0:T(8,128)(2,1)S(1)}, bf16[128,128]{1,0:T(8,128)(2,1)}, u32[]{:S(2)}) copy-start(bf16[128,128]{1,0:T(8,128)(2,1)} %param.14) | copy-start | bytes 98308
  14.2 109.0 %all-gather.3.cloned.1.call-start = ((), (), s32[]{:S(2)}) async-start(), calls=%async_computation | async-start | bytes 4718592 | tf_op jit(solution)/shard_map/all_gather | solution.py:45
  16.7 270.7 %all-reduce.3.cloned.1.call-start = ((), (), s32[]{:S(2)}) async-start(), calls=%async_computation.2 | async-start | bytes 16777216 | tf_op jit(solution)/shard_map/psum | solution.py:11
  76.2 0.8 copy-start.9
  307.3 7.4 %copy-start.6 = (f32[128]{0:T(128)S(1)}, f32[128]{0:T(128)}, u32[]{:S(2)}) copy-start(f32[128]{0:T(128)} %param.19) | copy-start | bytes 1540
  307.3 7.4 %copy-start.7 = (f32[128]{0:T(128)S(1)}, f32[128]{0:T(128)}, u32[]{:S(2)}) copy-start(f32[128]{0:T(128)} %param.18) | copy-start | bytes 1540
  314.2 0.8 copy-start.2
Sparse Core Ops, SparseCore 0:
  14.3 55.7 all-gather.4
  71.8 51.3 all-gather.2
  125.7 161.6 all-reduce.2
where the time goes:
time: 325 us; the launch traced here: 323 us
  waiting for transfers between devices  255 us (78%)
  local copies, waits for them, and re-layouts  21.1 us (6%)
  other arithmetic  17.4 us (5%)
  matrix products  16.1 us (5%)
  between operations  13.3 us (4%)
    psum x1, waiting for transfers between devices, spread(): return lax.psum(kept, axis)  156 us
    all_gather x1, waiting for transfers between devices, per_device(): lax.all_gather(right_proj, 'col', axis=2, tiled=True)  53.3 us
    all_gather x1, waiting for transfers between devices, per_device(): lax.all_gather(left_proj, 'col', axis=2, tiled=True)  45.4 us
    concatenate x1, local copies, waits for them, and re-layouts, per_device(): right_cols = jnp.concatenate(blocks, 1)  12.4 us
    all_gather x1, local copies, waits for them, and re-layouts, per_device(): lax.all_gather(left_proj, 'col', axis=2, tiled=True)  7.97 us
    concatenate x1, other arithmetic, per_device(): right_cols = jnp.concatenate(blocks, 1)  7.42 us
    dot_general x1, matrix products, per_device(): jnp.einsum('cik,cjk->cij', left_all, right_cols, preferred_element_type=j...  6.98 us
  transfers between devices with their start and end apart: 3, of which 3 were waited for; matrix products, arithmetic and copies ran while one was open for 5% of the time, Pallas kernels for 0%

commit v1 on v0

v1 whole, which is shorter than its diff:
```python
import jax
import jax.numpy as jnp
from jax import lax
from jax.experimental import pallas as pl
from jax.experimental.pallas import tpu as pltpu
from jax.sharding import PartitionSpec as P

EPS = 1e-05
CH = 128
ROWS, COLS = 32, 64
SLABS = ROWS * COLS // 128
HALF = ROWS // 2
POSITIONS = ROWS * COLS


def pair_positions(slab):
    return slab * COLS, HALF * COLS + slab * COLS


def input_norm(x_ref, gain, bias, slab):
    low, high = pair_positions(slab)
    values = jnp.concatenate([x_ref[pl.ds(low, COLS), :], x_ref[pl.ds(high, COLS), :]], 0)
    values = values.astype(jnp.float32)
    centred = values - jnp.mean(values, -1, keepdims=True)
    variance = jnp.mean(jnp.square(centred), -1, keepdims=True)
    return (centred * lax.rsqrt(variance + EPS) * gain + bias).astype(jnp.bfloat16)


def project_kernel(x_ref, gain_ref, bias_ref, wlg_ref, wl_ref, wrg_ref, wr_ref, out_ref, wide):
    weights = jnp.concatenate(
        [jnp.transpose(w_ref[...]) for w_ref in (wlg_ref, wl_ref, wrg_ref, wr_ref)], 0
    )
    gain, bias = gain_ref[...], bias_ref[...]
    for pair in range(SLABS // 2):
        normed = jnp.concatenate(
            [input_norm(x_ref, gain, bias, 2 * pair + member) for member in range(2)], 0
        )
        both = lax.dot_general(
            weights, normed, (((1,), (1,)), ((), ())), preferred_element_type=jnp.float32
        )
        left = jax.nn.sigmoid(both[:CH]) * both[CH : 2 * CH]
        right = jax.nn.sigmoid(both[2 * CH : 3 * CH]) * both[3 * CH :]
        for member in range(2):
            slab = 2 * pair + member
            lanes = slice(member * 128, member * 128 + 128)
            wide[pl.ds(slab, CH, stride=2 * SLABS), :] = left[:, lanes]
            wide[pl.ds(SLABS + slab, CH, stride=2 * SLABS), :] = right[:, lanes]
    out_ref[...] = wide[...].astype(jnp.bfloat16)


def gate_kernel(x_ref, gain_ref, bias_ref, w_ref, out_ref):
    gain, bias, weights = gain_ref[...], bias_ref[...], w_ref[...]
    for slab in range(SLABS):
        normed = input_norm(x_ref, gain, bias, slab)
        gate = jax.nn.sigmoid(jnp.dot(normed, weights, preferred_element_type=jnp.float32))
        low, high = pair_positions(slab)
        out_ref[pl.ds(low, COLS), :] = gate[:COLS]
        out_ref[pl.ds(high, COLS), :] = gate[COLS:]


def side_by_side(first, second, half):
    lanes = slice(half * 64, half * 64 + 64)
    return jnp.concatenate([first[:, lanes], second[:, lanes]], 1)


def mix_kernel(n_row, n_col, in_ref, out_ref, left, right):
    for r in range(n_row):
        for m in range(n_col // 2):
            start = (r * n_col + 2 * m) * 2 * SLABS
            first = in_ref[pl.ds(start, 2 * SLABS), :]
            second = in_ref[pl.ds(start + 2 * SLABS, 2 * SLABS), :]
            lanes = slice(m * 128, m * 128 + 128)
            for half in range(2):
                tile = side_by_side(first, second, half)
                rows = pl.ds(r * ROWS + half * HALF, HALF)
                left[rows, lanes] = tile[:SLABS]
                right[rows, lanes] = tile[SLABS:]
    for r in range(0, n_row, 4):
        block = lax.dot_general(
            left[pl.ds(r * ROWS, 4 * ROWS), :],
            right[...],
            (((1,), (1,)), ((), ())),
            preferred_element_type=jnp.float32,
        )
        for inner in range(4):
            for m in range(n_col // 2):
                lanes = slice(m * 128, m * 128 + 128)
                top = block[inner * ROWS : inner * ROWS + HALF, lanes]
                bottom = block[inner * ROWS + HALF : (inner + 1) * ROWS, lanes]
                for half in range(2):
                    start = ((r + inner) * n_col + 2 * m + half) * SLABS
                    out_ref[pl.ds(start, SLABS), :] = side_by_side(top, bottom, half).astype(
                        jnp.bfloat16
                    )


def finish_kernel(mixed_ref, gate_ref, gain_ref, bias_ref, w_ref, out_ref, wide):
    wide[...] = mixed_ref[...].astype(jnp.float32)
    total = jnp.zeros((SLABS, 128), jnp.float32)
    for c in range(CH):
        total += wide[pl.ds(c * SLABS, SLABS), :]
    mean = total / CH
    square = jnp.zeros((SLABS, 128), jnp.float32)
    for c in range(CH):
        square += jnp.square(wide[pl.ds(c * SLABS, SLABS), :] - mean)
    scale = lax.rsqrt(square / CH + EPS)
    gain = jnp.broadcast_to(gain_ref[...], (CH, 128))
    bias = jnp.broadcast_to(bias_ref[...], (CH, 128))
    weights = w_ref[...]
    for slab in range(SLABS):
        values = wide[pl.ds(slab, CH, stride=SLABS), :]
        normed = (values - mean[slab : slab + 1]) * scale[slab : slab + 1] * gain + bias
        projected = lax.dot_general(
            normed.astype(jnp.bfloat16),
            weights,
            (((0,), (0,)), ((), ())),
            preferred_element_type=jnp.float32,
        )
        low, high = pair_positions(slab)
        out_ref[pl.ds(low, COLS), :] = gate_ref[pl.ds(low, COLS), :] * projected[:COLS]
        out_ref[pl.ds(high, COLS), :] = gate_ref[pl.ds(high, COLS), :] * projected[COLS:]


def per_device(
    pair_rep,
    in_gain,
    in_bias,
    w_left_gate,
    w_left,
    w_right_gate,
    w_right,
    out_gain,
    out_bias,
    w_out_gate,
    w_out,
):
    n_row, n_col = lax.axis_size("row"), lax.axis_size("col")
    devices = n_row * n_col
    params = pltpu.CompilerParams(vmem_limit_bytes=48 << 20)
    flat = pair_rep.reshape(POSITIONS, CH)
    in_gain, in_bias = in_gain.reshape(1, CH), in_bias.reshape(1, CH)
    sent = pl.pallas_call(
        project_kernel,
        out_shape=jax.ShapeDtypeStruct((CH * 2 * SLABS, 128), jnp.bfloat16),
        scratch_shapes=[pltpu.VMEM((CH * 2 * SLABS, 128), jnp.float32)],
        compiler_params=params,
        name="project",
    )(flat, in_gain, in_bias, w_left_gate, w_left, w_right_gate, w_right)
    arrived = lax.all_to_all(
        sent.reshape(devices, 2 * SLABS, 128), ("row", "col"), 0, 0, tiled=True
    )
    gate_act = pl.pallas_call(
        gate_kernel,
        out_shape=jax.ShapeDtypeStruct((POSITIONS, CH), jnp.float32),
        compiler_params=params,
        cost_estimate=pl.CostEstimate(
            flops=2 * POSITIONS * CH * CH, bytes_accessed=3 << 19, transcendentals=POSITIONS * CH
        ),
        name="gate",
    )(flat, in_gain, in_bias, w_out_gate)
    n_res = n_row * ROWS
    mixed = pl.pallas_call(
        lambda *refs: mix_kernel(n_row, n_col, *refs),
        out_shape=jax.ShapeDtypeStruct((devices * SLABS, 128), jnp.bfloat16),
        scratch_shapes=[pltpu.VMEM((n_res, n_res), jnp.bfloat16)] * 2,
        compiler_params=params,
        name="mix",
    )(arrived.reshape(devices * 2 * SLABS, 128))
    returned = lax.all_to_all(
        mixed.reshape(devices, SLABS, 128), ("row", "col"), 0, 0, tiled=True
    )
    update = pl.pallas_call(
        finish_kernel,
        out_shape=jax.ShapeDtypeStruct((POSITIONS, CH), jnp.float32),
        scratch_shapes=[pltpu.VMEM((CH * SLABS, 128), jnp.float32)],
        compiler_params=params,
        name="finish",
    )(
        returned.reshape(CH * SLABS, 128),
        gate_act,
        out_gain.reshape(CH, 1),
        out_bias.reshape(CH, 1),
        w_out,
    )
    return update.reshape(ROWS, COLS, CH)


def solution(mesh):
    placed = (P("row", "col", None), P(), P(), P(), P(), P(), P(), P(), P(), P(), P())
    return jax.shard_map(
        per_device, mesh=mesh, in_specs=placed, out_specs=P("row", "col", None), check_vma=False
    )
```

time: 325 us -> 59.1 us (0.18)
  waiting for transfers between devices: 255 us -> 9.66 us
  blocking collectives: 0 us -> 29.7 us
  other arithmetic: 17.4 us -> 0 us
  matrix products: 16.1 us -> 0 us
  local copies, waits for them, and re-layouts: 21.1 us -> 6.92 us
  between operations: 13.3 us -> 0.05 us
  Pallas kernels: 0 us -> 7.18 us
  starting transfers between devices: 0.09 us -> 5 us
    psum x1 -> x0, waiting for transfers between devices: 156 us -> none  [spread(): return lax.psum(kept, axis)]
    all_gather x2 -> x0, waiting for transfers between devices: 98.8 us -> none  [the longest x1 53.3 us: per_device(): lax.all_gather(right_proj, 'col', axis=2, tiled=True)]
    all_to_all x0 -> x1, blocking collectives: none -> 29.7 us  [per_device(): lax.all_to_all(sent.reshape(devices, 2 * SLABS, 128), ('row', 'col'), 0,...]
    dot_general x7 -> x0, matrix products: 16.1 us -> none  [the longest x1 6.98 us: per_device(): jnp.einsum('cik,cjk->cij', left_all, right_cols, preferred_element_type=j...]
    concatenate x1 -> x0, local copies, waits for them, and re-layouts: 12.4 us -> none  [per_device(): right_cols = jnp.concatenate(blocks, 1)]
    all_to_all x0 -> x1, waiting for transfers between devices: none -> 9.66 us  [per_device(): lax.all_to_all(mixed.reshape(devices, SLABS, 128), ('row', 'col'), 0, 0,...]
    all_gather x1 -> x0, local copies, waits for them, and re-layouts: 7.97 us -> none  [per_device(): lax.all_gather(left_proj, 'col', axis=2, tiled=True)]
    concatenate x1 -> x0, other arithmetic: 7.42 us -> none  [per_device(): right_cols = jnp.concatenate(blocks, 1)]
  transfers between devices with their start and end apart: 3 -> 1, of which waited for: 3 -> 1; matrix products, arithmetic and copies ran while one was open for 5% -> 0% of each run, Pallas kernels for 0% -> 2%
where the time goes in v1:
time: 59.1 us; the launch traced here: 58.5 us
  blocking collectives  29.7 us (50%)
  waiting for transfers between devices  9.66 us (16%)
  Pallas kernels  7.18 us (12%)
  local copies, waits for them, and re-layouts  6.92 us (12%)
  starting transfers between devices  5 us (8%)
    all_to_all x1, blocking collectives, per_device(): lax.all_to_all(sent.reshape(devices, 2 * SLABS, 128), ('row', 'col'), 0,...  29.7 us
    all_to_all x1, waiting for transfers between devices, per_device(): lax.all_to_all(mixed.reshape(devices, SLABS, 128), ('row', 'col'), 0, 0,...  9.66 us
    unnamed x24, local copies, waits for them, and re-layouts  6.69 us
    all_to_all x1, starting transfers between devices, per_device(): lax.all_to_all(mixed.reshape(devices, SLABS, 128), ('row', 'col'), 0, 0,...  5 us
    pallas_call x1, Pallas kernels, per_device(): pl.pallas_call(project_kernel, out_shape=jax.ShapeDtypeStruct((CH * 2 * S...  2.34 us
    pallas_call x1, Pallas kernels, per_device(): pl.pallas_call(finish_kernel, out_shape=jax.ShapeDtypeStruct((POSITIONS,...  1.85 us
    pallas_call x1, Pallas kernels, per_device(): pl.pallas_call(lambda *refs: mix_kernel(n_row, n_col, *refs), out_shape=j...  1.82 us
  transfers between devices with their start and end apart: 1, of which 1 were waited for; matrix products, arithmetic and copies ran while one was open for 0% of the time, Pallas kernels for 2%

profile of v1, /device:TPU:1, one launch (start us, length us, event | category | flops | bytes accessed | tf_op | source)
XLA Modules:
  0.0 58.5 jit_solution(15472685117155660908)
XLA Ops:
  0.0 0.0 copy-start.8
  0.0 0.0 copy-start.9
  0.0 0.7 %copy-done.8 = f32[128]{0:T(128)S(1)} copy-done((f32[128]{0:T(128)S(1)}, f32[128]{0:T(128)}, u32[]{:S(2)}) %copy-start.8) | copy-done | bytes 536
  0.7 0.0 copy-done.9
  0.7 0.0 copy-start
  0.7 1.0 %copy-done = bf16[32,64,128]{2,1,0:T(8,128)(2,1)S(1)} copy-done((bf16[32,64,128]{2,1,0:T(8,128)(2,1)S(1)}, bf16[32,64,128]{2,1,0:T(8,128)(2,1)}, u32[]{:S(2)}) %copy-start) | copy-done | bytes 524312
  1.7 0.0 copy-start.3
  1.7 0.8 %copy-done.3 = bf16[128,128]{1,0:T(8,128)(2,1)S(1)} copy-done((bf16[128,128]{1,0:T(8,128)(2,1)S(1)}, bf16[128,128]{1,0:T(8,128)(2,1)}, u32[]{:S(2)}) %copy-start.3) | copy-done | bytes 32792
  2.5 0.8 %copy-done.4 = bf16[128,128]{1,0:T(8,128)(2,1)S(1)} copy-done((bf16[128,128]{1,0:T(8,128)(2,1)S(1)}, bf16[128,128]{1,0:T(8,128)(2,1)}, u32[]{:S(2)}) %copy-start.4) | copy-done | bytes 32792
  3.2 0.0 copy-start.5
  3.2 0.8 %copy-done.5 = bf16[128,128]{1,0:T(8,128)(2,1)S(1)} copy-done((bf16[128,128]{1,0:T(8,128)(2,1)S(1)}, bf16[128,128]{1,0:T(8,128)(2,1)}, u32[]{:S(2)}) %copy-start.5) | copy-done | bytes 32792
  4.0 0.0 copy-start.6
  4.0 0.8 %copy-done.6 = bf16[128,128]{1,0:T(8,128)(2,1)S(1)} copy-done((bf16[128,128]{1,0:T(8,128)(2,1)S(1)}, bf16[128,128]{1,0:T(8,128)(2,1)}, u32[]{:S(2)}) %copy-start.6) | copy-done | bytes 32792
  4.7 2.3 %project.1 = bf16[4096,128]{1,0:T(8,128)(2,1)S(1)} custom-call(bf16[2048,128]{1,0:T(8,128)(2,1)S(1)} %bitcast.12, f32[1,128]{1,0:T(1,128)S(1)} %bitcast.15, f32[1,128]{1,0:T(1,128)S(1)} %bitcast.17, bf16[128,128]{1,0:T(8,128)(2,1)S(1)} %copy-done.3, bf16[128,128]{1,0:T(8,128)(2,1)S(1)} %copy-done.4, bf16[128,128]{1,0:T(8,128)(2,1)S(1)} %copy-done.5, ...), custom_call_target="tpu_custom_call" | custom-call | tf_op jit(solution)/shard_map/project/pallas_call | solution.py:142
  7.1 29.7 %all_to_all.10 = bf16[128,32,128]{2,1,0:T(8,128)(2,1)S(1)} all-to-all(bf16[128,32,128]{2,1,0:T(8,128)(2,1)S(1)} %bitcast.11), channel_id=1, replica_groups=mesh['row'=16,'col'=8] {'row','col'}, dimensions={0} | all-to-all | bytes 2097152 | tf_op jit(solution)/shard_map/all_to_all | solution.py:149
  36.8 1.8 %mix.1 = bf16[2048,128]{1,0:T(8,128)(2,1)} custom-call(bf16[4096,128]{1,0:T(8,128)(2,1)S(1)} %bitcast.10), custom_call_target="tpu_custom_call" | custom-call | tf_op jit(solution)/shard_map/mix/pallas_call | solution.py:162
  38.6 0.0 copy-start.1
  38.6 5.0 %all-to-all-start.1 = ((bf16[128,16,128]{2,1,0:T(8,128)(2,1)}), bf16[128,16,128]{2,1,0:T(8,128)(2,1)S(1)}, u32[]{:S(2)}, u32[]{:S(2)}) async-start(bf16[128,16,128]{2,1,0:T(8,128)(2,1)} %bitcast.5), calls=%async_computation.1 | async-start | bytes 1048576 | tf_op jit(solution)/shard_map/all_to_all | solution.py:169
  43.6 0.0 copy-start.10
  43.7 0.6 %copy-done.10 = f32[128]{0:T(128)S(1)} copy-done((f32[128]{0:T(128)S(1)}, f32[128]{0:T(128)}, u32[]{:S(2)}) %copy-start.10) | copy-done | bytes 536
  44.3 0.1 copy.12.gain_ref
  44.4 0.0 copy-start.11
  44.4 0.7 %copy-done.11 = f32[128]{0:T(128)S(1)} copy-done((f32[128]{0:T(128)S(1)}, f32[128]{0:T(128)}, u32[]{:S(2)}) %copy-start.11) | copy-done | bytes 536
  45.1 0.0 copy-start.7
  45.1 0.1 copy.13.bias_ref
  45.2 0.0 copy-done.1
  45.2 0.6 %copy-done.7 = bf16[128,128]{1,0:T(8,128)(2,1)S(1)} copy-done((bf16[128,128]{1,0:T(8,128)(2,1)S(1)}, bf16[128,128]{1,0:T(8,128)(2,1)}, u32[]{:S(2)}) %copy-start.7) | copy-done | bytes 32792
  45.8 0.0 copy-start.2
  45.8 1.2 %gate.1.gate_ref = f32[2048,128]{1,0:T(8,128)S(1)} custom-call(bf16[2048,128]{1,0:T(8,128)(2,1)S(1)} %bitcast.13, f32[1,128]{1,0:T(1,128)S(1)} %bitcast.16, f32[1,128]{1,0:T(1,128)S(1)} %bitcast.18, bf16[128,128]{1,0:T(8,128)(2,1)S(1)} %copy-done.7), custom_call_target="tpu_custom_call" | custom-call | flops 67108864 | bytes 1572864 | tf_op jit(solution)/shard_map/gate/pallas_call | solution.py:152
  47.0 9.7 %all-to-all-done.1 = bf16[128,16,128]{2,1,0:T(8,128)(2,1)S(1)} async-done(((bf16[128,16,128]{2,1,0:T(8,128)(2,1)}), bf16[128,16,128]{2,1,0:T(8,128)(2,1)S(1)}, u32[]{:S(2)}, u32[]{:S(2)}) %all-to-all-start.1) | async-done | bytes 524320 | tf_op jit(solution)/shard_map/all_to_all | solution.py:169
  56.7 0.0 copy-done.2
  56.7 1.9 %finish.1 = f32[2048,128]{1,0:T(8,128)} custom-call(bf16[2048,128]{1,0:T(8,128)(2,1)S(1)} %bitcast.14, f32[2048,128]{1,0:T(8,128)S(1)} %gate.1.gate_ref, f32[128,1]{1,0:T(8,128)S(1)} %copy.12.gain_ref, f32[128,1]{1,0:T(8,128)S(1)} %copy.13.bias_ref, bf16[128,128]{1,0:T(8,128)(2,1)S(1)} %copy-done.2), custom_call_target="tpu_custom_call" | custom-call | tf_op jit(solution)/shard_map/finish/pallas_call | solution.py:172
  (1 shorter events, 0.0 us)
Async XLA Ops:
  0.0 0.7 %copy-start.8 = (f32[128]{0:T(128)S(1)}, f32[128]{0:T(128)}, u32[]{:S(2)}) copy-start(f32[128]{0:T(128)} %param.12) | copy-start | bytes 1540
  0.0 0.7 %copy-start.9 = (f32[128]{0:T(128)S(1)}, f32[128]{0:T(128)}, u32[]{:S(2)}) copy-start(f32[128]{0:T(128)} %param.13) | copy-start | bytes 1540
  0.7 1.0 %copy-start = (bf16[32,64,128]{2,1,0:T(8,128)(2,1)S(1)}, bf16[32,64,128]{2,1,0:T(8,128)(2,1)}, u32[]{:S(2)}) copy-start(bf16[32,64,128]{2,1,0:T(8,128)(2,1)} %param.11) | copy-start | bytes 1572868
  1.7 0.8 %copy-start.3 = (bf16[128,128]{1,0:T(8,128)(2,1)S(1)}, bf16[128,128]{1,0:T(8,128)(2,1)}, u32[]{:S(2)}) copy-start(bf16[128,128]{1,0:T(8,128)(2,1)} %wlg_ref.1) | copy-start | bytes 98308
  2.5 0.8 %copy-start.4 = (bf16[128,128]{1,0:T(8,128)(2,1)S(1)}, bf16[128,128]{1,0:T(8,128)(2,1)}, u32[]{:S(2)}) copy-start(bf16[128,128]{1,0:T(8,128)(2,1)} %wl_ref.1) | copy-start | bytes 98308
  3.2 0.8 %copy-start.5 = (bf16[128,128]{1,0:T(8,128)(2,1)S(1)}, bf16[128,128]{1,0:T(8,128)(2,1)}, u32[]{:S(2)}) copy-start(bf16[128,128]{1,0:T(8,128)(2,1)} %wrg_ref.1) | copy-start | bytes 98308
  4.0 0.8 %copy-start.6 = (bf16[128,128]{1,0:T(8,128)(2,1)S(1)}, bf16[128,128]{1,0:T(8,128)(2,1)}, u32[]{:S(2)}) copy-start(bf16[128,128]{1,0:T(8,128)(2,1)} %wr_ref.1) | copy-start | bytes 98308
  38.6 6.6 %copy-start.1 = (bf16[32,64,128]{2,1,0:T(8,128)(2,1)S(1)}, bf16[32,64,128]{2,1,0:T(8,128)(2,1)}, u32[]{:S(2)}) copy-start(bf16[32,64,128]{2,1,0:T(8,128)(2,1)} %param.11) | copy-start | bytes 1572868
  38.6 18.0 %all-to-all-start.1 = ((bf16[128,16,128]{2,1,0:T(8,128)(2,1)}), bf16[128,16,128]{2,1,0:T(8,128)(2,1)S(1)}, u32[]{:S(2)}, u32[]{:S(2)}) async-start(bf16[128,16,128]{2,1,0:T(8,128)(2,1)} %bitcast.5), calls=%async_computation.1 | async-start | bytes 1048576 | tf_op jit(solution)/shard_map/all_to_all | solution.py:169
  43.6 0.7 %copy-start.10 = (f32[128]{0:T(128)S(1)}, f32[128]{0:T(128)}, u32[]{:S(2)}) copy-start(f32[128]{0:T(128)} %param.18) | copy-start | bytes 1540
  44.4 0.7 %copy-start.11 = (f32[128]{0:T(128)S(1)}, f32[128]{0:T(128)}, u32[]{:S(2)}) copy-start(f32[128]{0:T(128)} %param.19) | copy-start | bytes 1540
  45.1 0.8 %copy-start.7 = (bf16[128,128]{1,0:T(8,128)(2,1)S(1)}, bf16[128,128]{1,0:T(8,128)(2,1)}, u32[]{:S(2)}) copy-start(bf16[128,128]{1,0:T(8,128)(2,1)} %w_ref.2) | copy-start | bytes 98308
  45.8 10.8 %copy-start.2 = (bf16[128,128]{1,0:T(8,128)(2,1)S(1)}, bf16[128,128]{1,0:T(8,128)(2,1)}, u32[]{:S(2)}) copy-start(bf16[128,128]{1,0:T(8,128)(2,1)} %w_ref.3) | copy-start | bytes 98308

commit v2 on v1

--- a/solution.py
+++ b/solution.py
@@ -11,6 +11,14 @@
 SLABS = ROWS * COLS // 128
 HALF = ROWS // 2
 POSITIONS = ROWS * COLS
+PITCH = 36
+OUT_PITCH = 20
+PIECES = 2
+PIECE_ROWS = POSITIONS // 2 // PIECES
+
+
+def in_hbm(array):
+    return pltpu.with_memory_space_constraint(array, pltpu.HBM)
 
 
 def pair_positions(slab):
@@ -26,14 +34,25 @@
     return (centred * lax.rsqrt(variance + EPS) * gain + bias).astype(jnp.bfloat16)
 
 
-def project_kernel(x_ref, gain_ref, bias_ref, wlg_ref, wl_ref, wrg_ref, wr_ref, out_ref, wide):
-    weights = jnp.concatenate(
-        [jnp.transpose(w_ref[...]) for w_ref in (wlg_ref, wl_ref, wrg_ref, wr_ref)], 0
-    )
-    gain, bias = gain_ref[...], bias_ref[...]
+def project_kernel(
+    x_hbm, gain_hbm, bias_hbm, wlg_hbm, wl_hbm, wrg_hbm, wr_hbm, out_ref, x, norm, kept, wide, sems
+):
+    copies = [
+        pltpu.make_async_copy(gain_hbm, norm.at[pl.ds(0, 1)], sems.at[0]),
+        pltpu.make_async_copy(bias_hbm, norm.at[pl.ds(1, 1)], sems.at[1]),
+    ]
+    for k, w_hbm in enumerate((wlg_hbm, wl_hbm, wrg_hbm, wr_hbm)):
+        copies.append(pltpu.make_async_copy(w_hbm, kept.at[k], sems.at[2 + k]))
+    pieces = [[pltpu.make_async_copy(x_hbm, x, sems.at[6])]]
+    for copy in pieces[0] + copies + sum(pieces[1:], []):
+        copy.start()
+    for copy in pieces[0] + copies:
+        copy.wait()
+    weights = jnp.concatenate([jnp.transpose(kept[k]) for k in range(4)], 0)
+    gain, bias = norm[0:1, :], norm[1:2, :]
     for pair in range(SLABS // 2):
         normed = jnp.concatenate(
-            [input_norm(x_ref, gain, bias, 2 * pair + member) for member in range(2)], 0
+            [input_norm(x, gain, bias, 2 * pair + member) for member in range(2)], 0
         )
         both = lax.dot_general(
             weights, normed, (((1,), (1,)), ((), ())), preferred_element_type=jnp.float32
@@ -43,9 +62,10 @@
         for member in range(2):
             slab = 2 * pair + member
             lanes = slice(member * 128, member * 128 + 128)
-            wide[pl.ds(slab, CH, stride=2 * SLABS), :] = left[:, lanes]
-            wide[pl.ds(SLABS + slab, CH, stride=2 * SLABS), :] = right[:, lanes]
-    out_ref[...] = wide[...].astype(jnp.bfloat16)
+            wide[pl.ds(slab, CH, stride=PITCH), :] = left[:, lanes]
+            wide[pl.ds(SLABS + slab, CH, stride=PITCH), :] = right[:, lanes]
+    for c in range(CH):
+        out_ref[pl.ds(c * 2 * SLABS, 2 * SLABS), :] = wide[pl.ds(c * PITCH, 2 * SLABS), :].astype(jnp.bfloat16)
 
 
 def gate_kernel(x_ref, gain_ref, bias_ref, w_ref, out_ref):
@@ -63,7 +83,8 @@
     return jnp.concatenate([first[:, lanes], second[:, lanes]], 1)
 
 
-def mix_kernel(n_row, n_col, in_ref, out_ref, left, right):
+def mix_kernel(n_row, n_col, in_ref, out_hbm, left, right, out_ref, sems):
+    copies = []
     for r in range(n_row):
         for m in range(n_col // 2):
             start = (r * n_col + 2 * m) * 2 * SLABS
@@ -92,23 +113,32 @@
                     out_ref[pl.ds(start, SLABS), :] = side_by_side(top, bottom, half).astype(
                         jnp.bfloat16
                     )
-
-
-def finish_kernel(mixed_ref, gate_ref, gain_ref, bias_ref, w_ref, out_ref, wide):
-    wide[...] = mixed_ref[...].astype(jnp.float32)
+        rows = pl.ds(r * n_col * SLABS, 4 * n_col * SLABS)
+        copies.append(pltpu.make_async_copy(out_ref.at[rows], out_hbm.at[rows], sems.at[r // 4]))
+        copies[-1].start()
+    for copy in copies:
+        copy.wait()
+
+
+def finish_kernel(
+    mixed_ref, gate_ref, gain_ref, bias_ref, w_ref, out_hbm, wide, out_ref, sems
+):
+    copies = []
+    for c in range(CH):
+        wide[pl.ds(c * OUT_PITCH, SLABS), :] = mixed_ref[pl.ds(c * SLABS, SLABS), :].astype(jnp.float32)
     total = jnp.zeros((SLABS, 128), jnp.float32)
     for c in range(CH):
-        total += wide[pl.ds(c * SLABS, SLABS), :]
+        total += wide[pl.ds(c * OUT_PITCH, SLABS), :]
     mean = total / CH
     square = jnp.zeros((SLABS, 128), jnp.float32)
     for c in range(CH):
-        square += jnp.square(wide[pl.ds(c * SLABS, SLABS), :] - mean)
+        square += jnp.square(wide[pl.ds(c * OUT_PITCH, SLABS), :] - mean)
     scale = lax.rsqrt(square / CH + EPS)
     gain = jnp.broadcast_to(gain_ref[...], (CH, 128))
     bias = jnp.broadcast_to(bias_ref[...], (CH, 128))
     weights = w_ref[...]
     for slab in range(SLABS):
-        values = wide[pl.ds(slab, CH, stride=SLABS), :]
+        values = wide[pl.ds(slab, CH, stride=OUT_PITCH), :]
         normed = (values - mean[slab : slab + 1]) * scale[slab : slab + 1] * gain + bias
         projected = lax.dot_general(
             normed.astype(jnp.bfloat16),
@@ -119,6 +149,17 @@
         low, high = pair_positions(slab)
         out_ref[pl.ds(low, COLS), :] = gate_ref[pl.ds(low, COLS), :] * projected[:COLS]
         out_ref[pl.ds(high, COLS), :] = gate_ref[pl.ds(high, COLS), :] * projected[COLS:]
+        if (slab + 1) % (SLABS // PIECES) == 0:
+            for half in range(2):
+                rows = pl.ds((half * PIECES + slab // (SLABS // PIECES)) * PIECE_ROWS, PIECE_ROWS)
+                copies.append(
+                    pltpu.make_async_copy(
+                        out_ref.at[rows], out_hbm.at[rows], sems.at[len(copies)]
+                    )
+                )
+                copies[-1].start()
+    for copy in copies:
+        copy.wait()
 
 
 def per_device(
@@ -142,10 +183,17 @@
     sent = pl.pallas_call(
         project_kernel,
         out_shape=jax.ShapeDtypeStruct((CH * 2 * SLABS, 128), jnp.bfloat16),
-        scratch_shapes=[pltpu.VMEM((CH * 2 * SLABS, 128), jnp.float32)],
+        in_specs=[pl.BlockSpec(memory_space=pltpu.HBM)] * 7,
+        scratch_shapes=[
+            pltpu.VMEM((POSITIONS, CH), jnp.bfloat16),
+            pltpu.VMEM((2, CH), jnp.float32),
+            pltpu.VMEM((4, CH, CH), jnp.bfloat16),
+            pltpu.VMEM((CH * PITCH, 128), jnp.float32),
+            pltpu.SemaphoreType.DMA((6 + 2 * PIECES,)),
+        ],
         compiler_params=params,
         name="project",
-    )(flat, in_gain, in_bias, w_left_gate, w_left, w_right_gate, w_right)
+    )(*map(in_hbm, (flat, in_gain, in_bias, w_left_gate, w_left, w_right_gate, w_right)))
     arrived = lax.all_to_all(
         sent.reshape(devices, 2 * SLABS, 128), ("row", "col"), 0, 0, tiled=True
     )
@@ -162,7 +210,13 @@
     mixed = pl.pallas_call(
         lambda *refs: mix_kernel(n_row, n_col, *refs),
         out_shape=jax.ShapeDtypeStruct((devices * SLABS, 128), jnp.bfloat16),
-        scratch_shapes=[pltpu.VMEM((n_res, n_res), jnp.bfloat16)] * 2,
+        out_specs=pl.BlockSpec(memory_space=pltpu.HBM),
+        scratch_shapes=[
+            pltpu.VMEM((n_res, n_res), jnp.bfloat16),
+            pltpu.VMEM((n_res, n_res), jnp.bfloat16),
+            pltpu.VMEM((devices * SLABS, 128), jnp.bfloat16),
+            pltpu.SemaphoreType.DMA((n_row // 4,)),
+        ],
         compiler_params=params,
         name="mix",
     )(arrived.reshape(devices * 2 * SLABS, 128))
@@ -172,7 +226,12 @@
     update = pl.pallas_call(
         finish_kernel,
         out_shape=jax.ShapeDtypeStruct((POSITIONS, CH), jnp.float32),
-        scratch_shapes=[pltpu.VMEM((CH * SLABS, 128), jnp.float32)],
+        out_specs=pl.BlockSpec(memory_space=pltpu.HBM),
+        scratch_shapes=[
+            pltpu.VMEM((CH * OUT_PITCH, 128), jnp.float32),
+            pltpu.VMEM((POSITIONS, CH), jnp.float32),
+            pltpu.SemaphoreType.DMA((2 * PIECES,)),
+        ],
         compiler_params=params,
         name="finish",
     )(

time: 59.1 us -> 53.8 us (0.910)
  local copies, waits for them, and re-layouts: 6.92 us -> 2.18 us
    unnamed x24 -> x14, local copies, waits for them, and re-layouts: 6.69 us -> 1.96 us
where the time goes in v2:
time: 53.8 us; the launch traced here: 53.5 us
  blocking collectives  29.7 us (55%)
  waiting for transfers between devices  9.67 us (18%)
  Pallas kernels  6.85 us (13%)
  starting transfers between devices  5.01 us (9%)
  local copies, waits for them, and re-layouts  2.18 us (4%)
    all_to_all x1, blocking collectives, per_device(): lax.all_to_all(sent.reshape(devices, 2 * SLABS, 128), ('row', 'col'), 0,...  29.7 us
    all_to_all x1, waiting for transfers between devices, per_device(): lax.all_to_all(mixed.reshape(devices, SLABS, 128), ('row', 'col'), 0, 0,...  9.67 us
    all_to_all x1, starting transfers between devices, per_device(): lax.all_to_all(mixed.reshape(devices, SLABS, 128), ('row', 'col'), 0, 0,...  5.01 us
    pallas_call x1, Pallas kernels, per_device(): pl.pallas_call(project_kernel, out_shape=jax.ShapeDtypeStruct((CH * 2 * S...  2.36 us
    unnamed x14, local copies, waits for them, and re-layouts  1.96 us
    pallas_call x1, Pallas kernels, per_device(): pl.pallas_call(lambda *refs: mix_kernel(n_row, n_col, *refs), out_shape=j...  1.72 us
    pallas_call x1, Pallas kernels, per_device(): pl.pallas_call(finish_kernel, out_shape=jax.ShapeDtypeStruct((POSITIONS,...  1.61 us
    pallas_call x1, Pallas kernels, per_device(): pl.pallas_call(gate_kernel, out_shape=jax.ShapeDtypeStruct((POSITIONS, CH...  1.17 us
  transfers between devices with their start and end apart: 1, of which 1 were waited for; matrix products, arithmetic and copies ran while one was open for 0% of the time, Pallas kernels for 2%

profile of v2, /device:TPU:1, one launch (start us, length us, event | category | flops | bytes accessed | tf_op | source)
XLA Modules:
  0.0 53.5 jit_solution(5740409382333452195)
XLA Ops:
  0.0 2.4 %project.1 = bf16[4096,128]{1,0:T(8,128)(2,1)S(1)} custom-call(bf16[2048,128]{1,0:T(8,128)(2,1)} %bitcast.12, f32[1,128]{1,0:T(1,128)} %bitcast.15, f32[1,128]{1,0:T(1,128)} %bitcast.17, bf16[128,128]{1,0:T(8,128)(2,1)} %wlg_hbm.1, bf16[128,128]{1,0:T(8,128)(2,1)} %wl_hbm.1, bf16[128,128]{1,0:T(8,128)(2,1)} %wrg_hbm.1, bf16[128,128]{1,0:T(8,128)(2,1)} %wr_hbm.1), custom_call_target="tpu_custom_call" | custom-call | tf_op jit(solution)/shard_map/project/pallas_call | solution.py:183
  2.4 29.7 %all_to_all.10 = bf16[128,32,128]{2,1,0:T(8,128)(2,1)S(1)} all-to-all(bf16[128,32,128]{2,1,0:T(8,128)(2,1)S(1)} %bitcast.11), channel_id=1, replica_groups=mesh['row'=16,'col'=8] {'row','col'}, dimensions={0} | all-to-all | bytes 2097152 | tf_op jit(solution)/shard_map/all_to_all | solution.py:197
  32.1 1.7 %mix.1 = bf16[2048,128]{1,0:T(8,128)(2,1)} custom-call(bf16[4096,128]{1,0:T(8,128)(2,1)S(1)} %bitcast.10), custom_call_target="tpu_custom_call" | custom-call | tf_op jit(solution)/shard_map/mix/pallas_call | solution.py:210
  33.8 0.0 copy-start
  33.8 5.0 %all-to-all-start.1 = ((bf16[128,16,128]{2,1,0:T(8,128)(2,1)}), bf16[128,16,128]{2,1,0:T(8,128)(2,1)S(1)}, u32[]{:S(2)}, u32[]{:S(2)}) async-start(bf16[128,16,128]{2,1,0:T(8,128)(2,1)} %bitcast.5), calls=%async_computation.1 | async-start | bytes 1048576 | tf_op jit(solution)/shard_map/all_to_all | solution.py:223
  38.8 0.0 copy-start.5
  38.8 0.6 %copy-done.5 = f32[128]{0:T(128)S(1)} copy-done((f32[128]{0:T(128)S(1)}, f32[128]{0:T(128)}, u32[]{:S(2)}) %copy-start.5) | copy-done | bytes 536
  39.5 0.1 copy.12.gain_ref
  39.6 0.0 copy-start.6
  39.6 0.7 %copy-done.6 = f32[128]{0:T(128)S(1)} copy-done((f32[128]{0:T(128)S(1)}, f32[128]{0:T(128)}, u32[]{:S(2)}) %copy-start.6) | copy-done | bytes 536
  40.3 0.0 copy-start.2
  40.3 0.0 copy-start.3
  40.3 0.0 copy-start.4
  40.3 0.1 copy.13.bias_ref
  40.4 0.0 copy-done
  40.4 0.6 %copy-done.2 = bf16[128,128]{1,0:T(8,128)(2,1)S(1)} copy-done((bf16[128,128]{1,0:T(8,128)(2,1)S(1)}, bf16[128,128]{1,0:T(8,128)(2,1)}, u32[]{:S(2)}) %copy-start.2) | copy-done | bytes 32792
  41.0 0.0 copy-done.3
  41.0 0.0 copy-done.4
  41.0 0.0 copy-start.1
  41.0 1.2 %gate.1.gate_ref = f32[2048,128]{1,0:T(8,128)S(1)} custom-call(bf16[2048,128]{1,0:T(8,128)(2,1)S(1)} %bitcast.13, f32[1,128]{1,0:T(1,128)S(1)} %bitcast.16, f32[1,128]{1,0:T(1,128)S(1)} %bitcast.18, bf16[128,128]{1,0:T(8,128)(2,1)S(1)} %copy-done.2), custom_call_target="tpu_custom_call" | custom-call | flops 67108864 | bytes 1572864 | tf_op jit(solution)/shard_map/gate/pallas_call | solution.py:200
  42.2 9.7 %all-to-all-done.1 = bf16[128,16,128]{2,1,0:T(8,128)(2,1)S(1)} async-done(((bf16[128,16,128]{2,1,0:T(8,128)(2,1)}), bf16[128,16,128]{2,1,0:T(8,128)(2,1)S(1)}, u32[]{:S(2)}, u32[]{:S(2)}) %all-to-all-start.1) | async-done | bytes 524320 | tf_op jit(solution)/shard_map/all_to_all | solution.py:223
  51.9 0.0 copy-done.1
  51.9 1.6 %finish.1 = f32[2048,128]{1,0:T(8,128)} custom-call(bf16[2048,128]{1,0:T(8,128)(2,1)S(1)} %bitcast.14, f32[2048,128]{1,0:T(8,128)S(1)} %gate.1.gate_ref, f32[128,1]{1,0:T(8,128)S(1)} %copy.12.gain_ref, f32[128,1]{1,0:T(8,128)S(1)} %copy.13.bias_ref, bf16[128,128]{1,0:T(8,128)(2,1)S(1)} %copy-done.1), custom_call_target="tpu_custom_call" | custom-call | tf_op jit(solution)/shard_map/finish/pallas_call | solution.py:226
Async XLA Ops:
  33.8 6.6 %copy-start = (bf16[32,64,128]{2,1,0:T(8,128)(2,1)S(1)}, bf16[32,64,128]{2,1,0:T(8,128)(2,1)}, u32[]{:S(2)}) copy-start(bf16[32,64,128]{2,1,0:T(8,128)(2,1)} %param.11) | copy-start | bytes 1572868
  33.8 18.1 %all-to-all-start.1 = ((bf16[128,16,128]{2,1,0:T(8,128)(2,1)}), bf16[128,16,128]{2,1,0:T(8,128)(2,1)S(1)}, u32[]{:S(2)}, u32[]{:S(2)}) async-start(bf16[128,16,128]{2,1,0:T(8,128)(2,1)} %bitcast.5), calls=%async_computation.1 | async-start | bytes 1048576 | tf_op jit(solution)/shard_map/all_to_all | solution.py:223
  38.8 0.7 %copy-start.5 = (f32[128]{0:T(128)S(1)}, f32[128]{0:T(128)}, u32[]{:S(2)}) copy-start(f32[128]{0:T(128)} %param.18) | copy-start | bytes 1540
  39.6 0.7 %copy-start.6 = (f32[128]{0:T(128)S(1)}, f32[128]{0:T(128)}, u32[]{:S(2)}) copy-start(f32[128]{0:T(128)} %param.19) | copy-start | bytes 1540
  40.3 0.8 %copy-start.2 = (bf16[128,128]{1,0:T(8,128)(2,1)S(1)}, bf16[128,128]{1,0:T(8,128)(2,1)}, u32[]{:S(2)}) copy-start(bf16[128,128]{1,0:T(8,128)(2,1)} %w_ref.2) | copy-start | bytes 98308
  40.3 0.8 %copy-start.3 = (f32[128]{0:T(128)S(1)}, f32[128]{0:T(128)}, u32[]{:S(2)}) copy-start(f32[128]{0:T(128)} %param.12) | copy-start | bytes 1540
  40.3 0.8 %copy-start.4 = (f32[128]{0:T(128)S(1)}, f32[128]{0:T(128)}, u32[]{:S(2)}) copy-start(f32[128]{0:T(128)} %param.13) | copy-start | bytes 1540
  41.0 10.8 %copy-start.1 = (bf16[128,128]{1,0:T(8,128)(2,1)S(1)}, bf16[128,128]{1,0:T(8,128)(2,1)}, u32[]{:S(2)}) copy-start(bf16[128,128]{1,0:T(8,128)(2,1)} %w_ref.3) | copy-start | bytes 98308

commit v3 on v2

--- a/solution.py
+++ b/solution.py
@@ -13,8 +13,6 @@
 POSITIONS = ROWS * COLS
 PITCH = 36
 OUT_PITCH = 20
-PIECES = 2
-PIECE_ROWS = POSITIONS // 2 // PIECES
 
 
 def in_hbm(array):
@@ -35,7 +33,7 @@
 
 
 def project_kernel(
-    x_hbm, gain_hbm, bias_hbm, wlg_hbm, wl_hbm, wrg_hbm, wr_hbm, out_ref, x, norm, kept, wide, sems
+    x_hbm, gain_hbm, bias_hbm, wlg_hbm, wl_hbm, wrg_hbm, wr_hbm, out_ref, normed_ref, x, norm, kept, wide, sems
 ):
     copies = [
         pltpu.make_async_copy(gain_hbm, norm.at[pl.ds(0, 1)], sems.at[0]),
@@ -54,6 +52,7 @@
         normed = jnp.concatenate(
             [input_norm(x, gain, bias, 2 * pair + member) for member in range(2)], 0
         )
+        normed_ref[pl.ds(pair * 256, 256), :] = normed
         both = lax.dot_general(
             weights, normed, (((1,), (1,)), ((), ())), preferred_element_type=jnp.float32
         )
@@ -68,23 +67,20 @@
         out_ref[pl.ds(c * 2 * SLABS, 2 * SLABS), :] = wide[pl.ds(c * PITCH, 2 * SLABS), :].astype(jnp.bfloat16)
 
 
-def gate_kernel(x_ref, gain_ref, bias_ref, w_ref, out_ref):
-    gain, bias, weights = gain_ref[...], bias_ref[...], w_ref[...]
-    for slab in range(SLABS):
-        normed = input_norm(x_ref, gain, bias, slab)
-        gate = jax.nn.sigmoid(jnp.dot(normed, weights, preferred_element_type=jnp.float32))
-        low, high = pair_positions(slab)
-        out_ref[pl.ds(low, COLS), :] = gate[:COLS]
-        out_ref[pl.ds(high, COLS), :] = gate[COLS:]
-
-
 def side_by_side(first, second, half):
     lanes = slice(half * 64, half * 64 + 64)
     return jnp.concatenate([first[:, lanes], second[:, lanes]], 1)
 
 
-def mix_kernel(n_row, n_col, in_ref, out_hbm, left, right, out_ref, sems):
-    copies = []
+def mix_kernel(
+    n_row, n_col, in_ref, gain_hbm, bias_hbm, out_ref, gain_ref, bias_ref, left, right, sems
+):
+    copies = [
+        pltpu.make_async_copy(gain_hbm, gain_ref, sems.at[0]),
+        pltpu.make_async_copy(bias_hbm, bias_ref, sems.at[1]),
+    ]
+    for copy in copies:
+        copy.start()
     for r in range(n_row):
         for m in range(n_col // 2):
             start = (r * n_col + 2 * m) * 2 * SLABS
@@ -113,19 +109,15 @@
                     out_ref[pl.ds(start, SLABS), :] = side_by_side(top, bottom, half).astype(
                         jnp.bfloat16
                     )
-        rows = pl.ds(r * n_col * SLABS, 4 * n_col * SLABS)
-        copies.append(pltpu.make_async_copy(out_ref.at[rows], out_hbm.at[rows], sems.at[r // 4]))
-        copies[-1].start()
     for copy in copies:
         copy.wait()
 
 
-def finish_kernel(
-    mixed_ref, gate_ref, gain_ref, bias_ref, w_ref, out_hbm, wide, out_ref, sems
-):
-    copies = []
-    for c in range(CH):
-        wide[pl.ds(c * OUT_PITCH, SLABS), :] = mixed_ref[pl.ds(c * SLABS, SLABS), :].astype(jnp.float32)
+def finish_kernel(mixed_ref, normed_ref, gain_ref, bias_ref, wg_ref, w_ref, out_hbm, wide, out_ref, sem):
+    for c in range(CH):
+        wide[pl.ds(c * OUT_PITCH, SLABS), :] = mixed_ref[pl.ds(c * SLABS, SLABS), :].astype(
+            jnp.float32
+        )
     total = jnp.zeros((SLABS, 128), jnp.float32)
     for c in range(CH):
         total += wide[pl.ds(c * OUT_PITCH, SLABS), :]
@@ -134,9 +126,9 @@
     for c in range(CH):
         square += jnp.square(wide[pl.ds(c * OUT_PITCH, SLABS), :] - mean)
     scale = lax.rsqrt(square / CH + EPS)
-    gain = jnp.broadcast_to(gain_ref[...], (CH, 128))
-    bias = jnp.broadcast_to(bias_ref[...], (CH, 128))
-    weights = w_ref[...]
+    gain = jnp.transpose(jnp.broadcast_to(gain_ref[...], (128, CH)))
+    bias = jnp.transpose(jnp.broadcast_to(bias_ref[...], (128, CH)))
+    gate_weights, weights = wg_ref[...], w_ref[...]
     for slab in range(SLABS):
         values = wide[pl.ds(slab, CH, stride=OUT_PITCH), :]
         normed = (values - mean[slab : slab + 1]) * scale[slab : slab + 1] * gain + bias
@@ -146,20 +138,16 @@
             (((0,), (0,)), ((), ())),
             preferred_element_type=jnp.float32,
         )
+        gate = jnp.dot(
+            normed_ref[pl.ds(slab * 128, 128), :], gate_weights, preferred_element_type=jnp.float32
+        )
+        update = jax.nn.sigmoid(gate) * projected
         low, high = pair_positions(slab)
-        out_ref[pl.ds(low, COLS), :] = gate_ref[pl.ds(low, COLS), :] * projected[:COLS]
-        out_ref[pl.ds(high, COLS), :] = gate_ref[pl.ds(high, COLS), :] * projected[COLS:]
-        if (slab + 1) % (SLABS // PIECES) == 0:
-            for half in range(2):
-                rows = pl.ds((half * PIECES + slab // (SLABS // PIECES)) * PIECE_ROWS, PIECE_ROWS)
-                copies.append(
-                    pltpu.make_async_copy(
-                        out_ref.at[rows], out_hbm.at[rows], sems.at[len(copies)]
-                    )
-                )
-                copies[-1].start()
-    for copy in copies:
-        copy.wait()
+        out_ref[pl.ds(low, COLS), :] = update[:COLS]
+        out_ref[pl.ds(high, COLS), :] = update[COLS:]
+    copy = pltpu.make_async_copy(out_ref, out_hbm, sem)
+    copy.start()
+    copy.wait()
 
 
 def per_device(
@@ -180,16 +168,19 @@
     params = pltpu.CompilerParams(vmem_limit_bytes=48 << 20)
     flat = pair_rep.reshape(POSITIONS, CH)
     in_gain, in_bias = in_gain.reshape(1, CH), in_bias.reshape(1, CH)
-    sent = pl.pallas_call(
+    sent, normed = pl.pallas_call(
         project_kernel,
-        out_shape=jax.ShapeDtypeStruct((CH * 2 * SLABS, 128), jnp.bfloat16),
+        out_shape=(
+            jax.ShapeDtypeStruct((CH * 2 * SLABS, 128), jnp.bfloat16),
+            jax.ShapeDtypeStruct((POSITIONS, CH), jnp.bfloat16),
+        ),
         in_specs=[pl.BlockSpec(memory_space=pltpu.HBM)] * 7,
         scratch_shapes=[
             pltpu.VMEM((POSITIONS, CH), jnp.bfloat16),
             pltpu.VMEM((2, CH), jnp.float32),
             pltpu.VMEM((4, CH, CH), jnp.bfloat16),
             pltpu.VMEM((CH * PITCH, 128), jnp.float32),
-            pltpu.SemaphoreType.DMA((6 + 2 * PIECES,)),
+            pltpu.SemaphoreType.DMA((7,)),
         ],
         compiler_params=params,
         name="project",
@@ -197,29 +188,27 @@
     arrived = lax.all_to_all(
         sent.reshape(devices, 2 * SLABS, 128), ("row", "col"), 0, 0, tiled=True
     )
-    gate_act = pl.pallas_call(
-        gate_kernel,
-        out_shape=jax.ShapeDtypeStruct((POSITIONS, CH), jnp.float32),
-        compiler_params=params,
-        cost_estimate=pl.CostEstimate(
-            flops=2 * POSITIONS * CH * CH, bytes_accessed=3 << 19, transcendentals=POSITIONS * CH
+    n_res = n_row * ROWS
+    mixed, out_gain, out_bias = pl.pallas_call(
+        lambda *refs: mix_kernel(n_row, n_col, *refs),
+        out_shape=(
+            jax.ShapeDtypeStruct((devices * SLABS, 128), jnp.bfloat16),
+            jax.ShapeDtypeStruct((1, CH), jnp.float32),
+            jax.ShapeDtypeStruct((1, CH), jnp.float32),
         ),
-        name="gate",
-    )(flat, in_gain, in_bias, w_out_gate)
-    n_res = n_row * ROWS
-    mixed = pl.pallas_call(
-        lambda *refs: mix_kernel(n_row, n_col, *refs),
-        out_shape=jax.ShapeDtypeStruct((devices * SLABS, 128), jnp.bfloat16),
-        out_specs=pl.BlockSpec(memory_space=pltpu.HBM),
+        in_specs=[pl.BlockSpec(memory_space=space) for space in (pltpu.VMEM, pltpu.HBM, pltpu.HBM)],
         scratch_shapes=[
             pltpu.VMEM((n_res, n_res), jnp.bfloat16),
             pltpu.VMEM((n_res, n_res), jnp.bfloat16),
-            pltpu.VMEM((devices * SLABS, 128), jnp.bfloat16),
-            pltpu.SemaphoreType.DMA((n_row // 4,)),
+            pltpu.SemaphoreType.DMA((2,)),
         ],
         compiler_params=params,
         name="mix",
-    )(arrived.reshape(devices * 2 * SLABS, 128))
+    )(
+        arrived.reshape(devices * 2 * SLABS, 128),
+        in_hbm(out_gain.reshape(1, CH)),
+        in_hbm(out_bias.reshape(1, CH)),
+    )
     returned = lax.all_to_all(
         mixed.reshape(devices, SLABS, 128), ("row", "col"), 0, 0, tiled=True
     )
@@ -230,15 +219,16 @@
         scratch_shapes=[
             pltpu.VMEM((CH * OUT_PITCH, 128), jnp.float32),
             pltpu.VMEM((POSITIONS, CH), jnp.float32),
-            pltpu.SemaphoreType.DMA((2 * PIECES,)),
+            pltpu.SemaphoreType.DMA,
         ],
         compiler_params=params,
         name="finish",
     )(
         returned.reshape(CH * SLABS, 128),
-        gate_act,
-        out_gain.reshape(CH, 1),
-        out_bias.reshape(CH, 1),
+        normed,
+        out_gain,
+        out_bias,
+        w_out_gate,
         w_out,
     )
     return update.reshape(ROWS, COLS, CH)

time: 53.8 us -> 52.9 us (0.983)
  blocking collectives: 29.7 us -> 47.4 us
  waiting for transfers between devices: 9.67 us -> 0 us
  starting transfers between devices: 5.01 us -> 0 us
  local copies, waits for them, and re-layouts: 2.18 us -> 0.01 us
  Pallas kernels: 6.85 us -> 5.22 us
    all_to_all x0 -> x1, blocking collectives: none -> 17.7 us  [per_device(): lax.all_to_all(mixed.reshape(devices, SLABS, 128), ('row', 'col'), 0, 0,...]
    all_to_all x1 -> x0, waiting for transfers between devices: 9.67 us -> none  [per_device(): lax.all_to_all(mixed.reshape(devices, SLABS, 128), ('row', 'col'), 0, 0,...]
    all_to_all x1 -> x0, starting transfers between devices: 5.01 us -> none  [per_device(): lax.all_to_all(mixed.reshape(devices, SLABS, 128), ('row', 'col'), 0, 0,...]
    unnamed x14 -> x4, local copies, waits for them, and re-layouts: 1.96 us -> 0.01 us
    pallas_call x3 -> x2, Pallas kernels: 5.24 us -> 3.38 us  [the longest x1 2.32 us: per_device(): pl.pallas_call(project_kernel, out_shape=(jax.ShapeDtypeStruct((CH * 2 *...]
  transfers between devices with their start and end apart: 1 -> 0, of which waited for: 1 -> 0; matrix products, arithmetic and copies ran while one was open for 0% -> 0% of each run, Pallas kernels for 2% -> 0%
where the time goes in v3:
time: 52.9 us; the launch traced here: 52.7 us
  blocking collectives  47.4 us (90%)
  Pallas kernels  5.22 us (10%)
    all_to_all x1, blocking collectives, per_device(): lax.all_to_all(sent.reshape(devices, 2 * SLABS, 128), ('row', 'col'), 0,...  29.7 us
    all_to_all x1, blocking collectives, per_device(): lax.all_to_all(mixed.reshape(devices, SLABS, 128), ('row', 'col'), 0, 0,...  17.7 us
    pallas_call x1, Pallas kernels, per_device(): pl.pallas_call(project_kernel, out_shape=(jax.ShapeDtypeStruct((CH * 2 *...  2.32 us
    pallas_call x1, Pallas kernels, per_device(): pl.pallas_call(finish_kernel, out_shape=jax.ShapeDtypeStruct((POSITIONS,...  1.84 us

profile of v3, /device:TPU:1, one launch (start us, length us, event | category | flops | bytes accessed | tf_op | source)
XLA Modules:
  0.0 52.7 jit_solution(8638187633914214754)
XLA Ops:
  0.0 2.3 %project.1 = (bf16[4096,128]{1,0:T(8,128)(2,1)S(1)}, bf16[2048,128]{1,0:T(8,128)(2,1)S(1)}) custom-call(bf16[2048,128]{1,0:T(8,128)(2,1)} %bitcast.14, f32[1,128]{1,0:T(1,128)} %bitcast.17, f32[1,128]{1,0:T(1,128)} %bitcast.18, bf16[128,128]{1,0:T(8,128)(2,1)} %wlg_hbm.1, bf16[128,128]{1,0:T(8,128)(2,1)} %wl_hbm.1, bf16[128,128]{1,0:T(8,128)(2,1)} %wrg_hbm.1, ...), custom_call_target="tpu_custom_call" | custom-call | tf_op jit(solution)/shard_map/project/pallas_call | solution.py:171
  2.3 29.7 %all_to_all.10 = bf16[128,32,128]{2,1,0:T(8,128)(2,1)S(1)} all-to-all(bf16[128,32,128]{2,1,0:T(8,128)(2,1)S(1)} %bitcast.12), channel_id=1, replica_groups=mesh['row'=16,'col'=8] {'row','col'}, dimensions={0} | all-to-all | bytes 2097152 | tf_op jit(solution)/shard_map/all_to_all | solution.py:188
  32.1 1.1 %mix.1 = (bf16[2048,128]{1,0:T(8,128)(2,1)S(1)}, f32[1,128]{1,0:T(1,128)S(1)}, f32[1,128]{1,0:T(1,128)S(1)}) custom-call(bf16[4096,128]{1,0:T(8,128)(2,1)S(1)} %bitcast.10, f32[1,128]{1,0:T(1,128)} %bitcast.15, f32[1,128]{1,0:T(1,128)} %bitcast.16), custom_call_target="tpu_custom_call" | custom-call | tf_op jit(solution)/shard_map/mix/pallas_call | solution.py:192
  33.1 0.0 copy-start
  33.1 0.0 copy-start.1
  33.1 17.7 %all_to_all.11 = bf16[128,16,128]{2,1,0:T(8,128)(2,1)S(1)} all-to-all(bf16[128,16,128]{2,1,0:T(8,128)(2,1)S(1)} %bitcast.13), channel_id=1, replica_groups=mesh['row'=16,'col'=8] {'row','col'}, dimensions={0} | all-to-all | bytes 1048576 | tf_op jit(solution)/shard_map/all_to_all | solution.py:212
  50.9 0.0 copy-done
  50.9 0.0 copy-done.1
  50.9 1.8 %finish.1 = f32[2048,128]{1,0:T(8,128)} custom-call(bf16[2048,128]{1,0:T(8,128)(2,1)S(1)} %bitcast.11, bf16[2048,128]{1,0:T(8,128)(2,1)S(1)} %get-tuple-element.12.normed_ref, f32[1,128]{1,0:T(1,128)S(1)} %get-tuple-element.13.gain_ref, f32[1,128]{1,0:T(1,128)S(1)} %get-tuple-element.14.bias_ref, bf16[128,128]{1,0:T(8,128)(2,1)S(1)} %copy-done, ...), custom_call_target="tpu_custom_call" | custom-call | tf_op jit(solution)/shard_map/finish/pallas_call | solution.py:215
Async XLA Ops:
  33.1 17.7 %copy-start = (bf16[128,128]{1,0:T(8,128)(2,1)S(1)}, bf16[128,128]{1,0:T(8,128)(2,1)}, u32[]{:S(2)}) copy-start(bf16[128,128]{1,0:T(8,128)(2,1)} %wg_ref.1) | copy-start | bytes 98308
  33.1 17.7 %copy-start.1 = (bf16[128,128]{1,0:T(8,128)(2,1)S(1)}, bf16[128,128]{1,0:T(8,128)(2,1)}, u32[]{:S(2)}) copy-start(bf16[128,128]{1,0:T(8,128)(2,1)} %w_ref.1) | copy-start | bytes 98308

commit v4 on v3

--- a/solution.py
+++ b/solution.py
@@ -41,13 +41,14 @@
     ]
     for k, w_hbm in enumerate((wlg_hbm, wl_hbm, wrg_hbm, wr_hbm)):
         copies.append(pltpu.make_async_copy(w_hbm, kept.at[k], sems.at[2 + k]))
-    pieces = [[pltpu.make_async_copy(x_hbm, x, sems.at[6])]]
-    for copy in pieces[0] + copies + sum(pieces[1:], []):
+    copy_x = pltpu.make_async_copy(x_hbm, x, sems.at[6])
+    for copy in [copy_x] + copies:
         copy.start()
-    for copy in pieces[0] + copies:
+    for copy in copies:
         copy.wait()
     weights = jnp.concatenate([jnp.transpose(kept[k]) for k in range(4)], 0)
     gain, bias = norm[0:1, :], norm[1:2, :]
+    copy_x.wait()
     for pair in range(SLABS // 2):
         normed = jnp.concatenate(
             [input_norm(x, gain, bias, 2 * pair + member) for member in range(2)], 0
@@ -92,14 +93,14 @@
                 rows = pl.ds(r * ROWS + half * HALF, HALF)
                 left[rows, lanes] = tile[:SLABS]
                 right[rows, lanes] = tile[SLABS:]
-    for r in range(0, n_row, 4):
+    for r in range(0, n_row, 8):
         block = lax.dot_general(
-            left[pl.ds(r * ROWS, 4 * ROWS), :],
+            left[pl.ds(r * ROWS, 8 * ROWS), :],
             right[...],
             (((1,), (1,)), ((), ())),
             preferred_element_type=jnp.float32,
         )
-        for inner in range(4):
+        for inner in range(8):
             for m in range(n_col // 2):
                 lanes = slice(m * 128, m * 128 + 128)
                 top = block[inner * ROWS : inner * ROWS + HALF, lanes]

time: 52.9 us -> 52.5 us (level)
  no operation moved by 1% of the time
where the time goes in v4:
time: 52.5 us; the launch traced here: 52.3 us
  blocking collectives  47.4 us (90%)
  Pallas kernels  4.84 us (9%)
    all_to_all x1, blocking collectives, per_device(): lax.all_to_all(sent.reshape(devices, 2 * SLABS, 128), ('row', 'col'), 0,...  29.7 us
    all_to_all x1, blocking collectives, per_device(): lax.all_to_all(mixed.reshape(devices, SLABS, 128), ('row', 'col'), 0, 0,...  17.7 us
    pallas_call x1, Pallas kernels, per_device(): pl.pallas_call(project_kernel, out_shape=(jax.ShapeDtypeStruct((CH * 2 *...  2.25 us
    pallas_call x1, Pallas kernels, per_device(): pl.pallas_call(finish_kernel, out_shape=jax.ShapeDtypeStruct((POSITIONS,...  1.84 us

profile of v4, /device:TPU:1, one launch (start us, length us, event | category | flops | bytes accessed | tf_op | source)
XLA Modules:
  0.0 52.3 jit_solution(8389772832091716740)
XLA Ops:
  0.0 2.3 %project.1 = (bf16[4096,128]{1,0:T(8,128)(2,1)S(1)}, bf16[2048,128]{1,0:T(8,128)(2,1)S(1)}) custom-call(bf16[2048,128]{1,0:T(8,128)(2,1)} %bitcast.14, f32[1,128]{1,0:T(1,128)} %bitcast.17, f32[1,128]{1,0:T(1,128)} %bitcast.18, bf16[128,128]{1,0:T(8,128)(2,1)} %wlg_hbm.1, bf16[128,128]{1,0:T(8,128)(2,1)} %wl_hbm.1, bf16[128,128]{1,0:T(8,128)(2,1)} %wrg_hbm.1, ...), custom_call_target="tpu_custom_call" | custom-call | tf_op jit(solution)/shard_map/project/pallas_call | solution.py:172
  2.3 29.7 %all_to_all.10 = bf16[128,32,128]{2,1,0:T(8,128)(2,1)S(1)} all-to-all(bf16[128,32,128]{2,1,0:T(8,128)(2,1)S(1)} %bitcast.12), channel_id=1, replica_groups=mesh['row'=16,'col'=8] {'row','col'}, dimensions={0} | all-to-all | bytes 2097152 | tf_op jit(solution)/shard_map/all_to_all | solution.py:189
  32.0 0.7 %mix.1 = (bf16[2048,128]{1,0:T(8,128)(2,1)S(1)}, f32[1,128]{1,0:T(1,128)S(1)}, f32[1,128]{1,0:T(1,128)S(1)}) custom-call(bf16[4096,128]{1,0:T(8,128)(2,1)S(1)} %bitcast.10, f32[1,128]{1,0:T(1,128)} %bitcast.15, f32[1,128]{1,0:T(1,128)} %bitcast.16), custom_call_target="tpu_custom_call" | custom-call | tf_op jit(solution)/shard_map/mix/pallas_call | solution.py:193
  32.7 0.0 copy-start
  32.7 0.0 copy-start.1
  32.8 17.7 %all_to_all.11 = bf16[128,16,128]{2,1,0:T(8,128)(2,1)S(1)} all-to-all(bf16[128,16,128]{2,1,0:T(8,128)(2,1)S(1)} %bitcast.13), channel_id=1, replica_groups=mesh['row'=16,'col'=8] {'row','col'}, dimensions={0} | all-to-all | bytes 1048576 | tf_op jit(solution)/shard_map/all_to_all | solution.py:213
  50.5 0.0 copy-done
  50.5 0.0 copy-done.1
  50.5 1.8 %finish.1 = f32[2048,128]{1,0:T(8,128)} custom-call(bf16[2048,128]{1,0:T(8,128)(2,1)S(1)} %bitcast.11, bf16[2048,128]{1,0:T(8,128)(2,1)S(1)} %get-tuple-element.12.normed_ref, f32[1,128]{1,0:T(1,128)S(1)} %get-tuple-element.13.gain_ref, f32[1,128]{1,0:T(1,128)S(1)} %get-tuple-element.14.bias_ref, bf16[128,128]{1,0:T(8,128)(2,1)S(1)} %copy-done, ...), custom_call_target="tpu_custom_call" | custom-call | tf_op jit(solution)/shard_map/finish/pallas_call | solution.py:216
Async XLA Ops:
  32.7 17.7 %copy-start = (bf16[128,128]{1,0:T(8,128)(2,1)S(1)}, bf16[128,128]{1,0:T(8,128)(2,1)}, u32[]{:S(2)}) copy-start(bf16[128,128]{1,0:T(8,128)(2,1)} %wg_ref.1) | copy-start | bytes 98308
  32.7 17.7 %copy-start.1 = (bf16[128,128]{1,0:T(8,128)(2,1)S(1)}, bf16[128,128]{1,0:T(8,128)(2,1)}, u32[]{:S(2)}) copy-start(bf16[128,128]{1,0:T(8,128)(2,1)} %w_ref.1) | copy-start | bytes 98308

commit v5 on v4

--- a/solution.py
+++ b/solution.py
@@ -115,40 +115,54 @@
 
 
 def finish_kernel(mixed_ref, normed_ref, gain_ref, bias_ref, wg_ref, w_ref, out_hbm, wide, out_ref, sem):
+    total = [jnp.zeros((SLABS, 128), jnp.float32)] * 8
     for c in range(CH):
-        wide[pl.ds(c * OUT_PITCH, SLABS), :] = mixed_ref[pl.ds(c * SLABS, SLABS), :].astype(
-            jnp.float32
-        )
-    total = jnp.zeros((SLABS, 128), jnp.float32)
+        values = mixed_ref[pl.ds(c * SLABS, SLABS), :].astype(jnp.float32)
+        wide[pl.ds(c * OUT_PITCH, SLABS), :] = values
+        total[c % 8] += values
+    mean = sum(total[1:], total[0]) / CH
+    square = [jnp.zeros((SLABS, 128), jnp.float32)] * 8
     for c in range(CH):
-        total += wide[pl.ds(c * OUT_PITCH, SLABS), :]
-    mean = total / CH
-    square = jnp.zeros((SLABS, 128), jnp.float32)
-    for c in range(CH):
-        square += jnp.square(wide[pl.ds(c * OUT_PITCH, SLABS), :] - mean)
-    scale = lax.rsqrt(square / CH + EPS)
+        values = mixed_ref[pl.ds(c * SLABS, SLABS), :].astype(jnp.float32)
+        square[c % 8] += jnp.square(values - mean)
+    scale = lax.rsqrt(sum(square[1:], square[0]) / CH + EPS)
     gain = jnp.transpose(jnp.broadcast_to(gain_ref[...], (128, CH)))
     bias = jnp.transpose(jnp.broadcast_to(bias_ref[...], (128, CH)))
     gate_weights, weights = wg_ref[...], w_ref[...]
-    for slab in range(SLABS):
-        values = wide[pl.ds(slab, CH, stride=OUT_PITCH), :]
-        normed = (values - mean[slab : slab + 1]) * scale[slab : slab + 1] * gain + bias
+    copies = []
+    for first in range(0, SLABS, 4):
+        columns = []
+        for slab in range(first, first + 4):
+            values = wide[pl.ds(slab, CH, stride=OUT_PITCH), :]
+            normed = (values - mean[slab : slab + 1]) * scale[slab : slab + 1] * gain + bias
+            columns.append(normed.astype(jnp.bfloat16))
         projected = lax.dot_general(
-            normed.astype(jnp.bfloat16),
+            jnp.concatenate(columns, 1),
             weights,
             (((0,), (0,)), ((), ())),
             preferred_element_type=jnp.float32,
         )
         gate = jnp.dot(
-            normed_ref[pl.ds(slab * 128, 128), :], gate_weights, preferred_element_type=jnp.float32
+            normed_ref[pl.ds(first * 128, 4 * 128), :],
+            gate_weights,
+            preferred_element_type=jnp.float32,
         )
         update = jax.nn.sigmoid(gate) * projected
-        low, high = pair_positions(slab)
-        out_ref[pl.ds(low, COLS), :] = update[:COLS]
-        out_ref[pl.ds(high, COLS), :] = update[COLS:]
-    copy = pltpu.make_async_copy(out_ref, out_hbm, sem)
-    copy.start()
-    copy.wait()
+        for member in range(4):
+            low, high = pair_positions(first + member)
+            middle = member * 128 + COLS
+            out_ref[pl.ds(low, COLS), :] = update[middle - COLS : middle]
+            out_ref[pl.ds(high, COLS), :] = update[middle : middle + COLS]
+        if first + 4 in (8, SLABS):
+            begin = 0 if first + 4 == 8 else 8
+            for start in pair_positions(begin):
+                rows = pl.ds(start, (first + 4 - begin) * COLS)
+                copies.append(
+                    pltpu.make_async_copy(out_ref.at[rows], out_hbm.at[rows], sem.at[len(copies)])
+                )
+                copies[-1].start()
+    for copy in copies:
+        copy.wait()
 
 
 def per_device(
@@ -180,7 +194,7 @@
             pltpu.VMEM((POSITIONS, CH), jnp.bfloat16),
             pltpu.VMEM((2, CH), jnp.float32),
             pltpu.VMEM((4, CH, CH), jnp.bfloat16),
-            pltpu.VMEM((CH * PITCH, 128), jnp.float32),
+            pltpu.VMEM(((CH + 2) * PITCH, 128), jnp.float32),
             pltpu.SemaphoreType.DMA((7,)),
         ],
         compiler_params=params,
@@ -218,9 +232,9 @@
         out_shape=jax.ShapeDtypeStruct((POSITIONS, CH), jnp.float32),
         out_specs=pl.BlockSpec(memory_space=pltpu.HBM),
         scratch_shapes=[
-            pltpu.VMEM((CH * OUT_PITCH, 128), jnp.float32),
+            pltpu.VMEM(((CH + 2) * OUT_PITCH, 128), jnp.float32),
             pltpu.VMEM((POSITIONS, CH), jnp.float32),
-            pltpu.SemaphoreType.DMA,
+            pltpu.SemaphoreType.DMA((4,)),
         ],
         compiler_params=params,
         name="finish",

time: 52.5 us -> 52.2 us (level)
  no operation moved by 1% of the time
where the time goes in v5:
time: 52.2 us; the launch traced here: 52 us
  blocking collectives  47.4 us (91%)
  Pallas kernels  4.53 us (9%)
    all_to_all x1, blocking collectives, per_device(): lax.all_to_all(sent.reshape(devices, 2 * SLABS, 128), ('row', 'col'), 0,...  29.7 us
    all_to_all x1, blocking collectives, per_device(): lax.all_to_all(mixed.reshape(devices, SLABS, 128), ('row', 'col'), 0, 0,...  17.7 us
    pallas_call x1, Pallas kernels, per_device(): pl.pallas_call(project_kernel, out_shape=(jax.ShapeDtypeStruct((CH * 2 *...  2.25 us
    pallas_call x1, Pallas kernels, per_device(): pl.pallas_call(finish_kernel, out_shape=jax.ShapeDtypeStruct((POSITIONS,...  1.53 us

profile of v5, /device:TPU:1, one launch (start us, length us, event | category | flops | bytes accessed | tf_op | source)
XLA Modules:
  0.0 52.0 jit_solution(14421591074402231655)
XLA Ops:
  0.0 2.3 %project.1 = (bf16[4096,128]{1,0:T(8,128)(2,1)S(1)}, bf16[2048,128]{1,0:T(8,128)(2,1)S(1)}) custom-call(bf16[2048,128]{1,0:T(8,128)(2,1)} %bitcast.14, f32[1,128]{1,0:T(1,128)} %bitcast.17, f32[1,128]{1,0:T(1,128)} %bitcast.18, bf16[128,128]{1,0:T(8,128)(2,1)} %wlg_hbm.1, bf16[128,128]{1,0:T(8,128)(2,1)} %wl_hbm.1, bf16[128,128]{1,0:T(8,128)(2,1)} %wrg_hbm.1, ...), custom_call_target="tpu_custom_call" | custom-call | tf_op jit(solution)/shard_map/project/pallas_call | solution.py:186
  2.3 29.7 %all_to_all.10 = bf16[128,32,128]{2,1,0:T(8,128)(2,1)S(1)} all-to-all(bf16[128,32,128]{2,1,0:T(8,128)(2,1)S(1)} %bitcast.12), channel_id=1, replica_groups=mesh['row'=16,'col'=8] {'row','col'}, dimensions={0} | all-to-all | bytes 2097152 | tf_op jit(solution)/shard_map/all_to_all | solution.py:203
  32.0 0.7 %mix.1 = (bf16[2048,128]{1,0:T(8,128)(2,1)S(1)}, f32[1,128]{1,0:T(1,128)S(1)}, f32[1,128]{1,0:T(1,128)S(1)}) custom-call(bf16[4096,128]{1,0:T(8,128)(2,1)S(1)} %bitcast.10, f32[1,128]{1,0:T(1,128)} %bitcast.15, f32[1,128]{1,0:T(1,128)} %bitcast.16), custom_call_target="tpu_custom_call" | custom-call | tf_op jit(solution)/shard_map/mix/pallas_call | solution.py:207
  32.7 0.0 copy-start
  32.7 0.0 copy-start.1
  32.8 17.7 %all_to_all.11 = bf16[128,16,128]{2,1,0:T(8,128)(2,1)S(1)} all-to-all(bf16[128,16,128]{2,1,0:T(8,128)(2,1)S(1)} %bitcast.13), channel_id=1, replica_groups=mesh['row'=16,'col'=8] {'row','col'}, dimensions={0} | all-to-all | bytes 1048576 | tf_op jit(solution)/shard_map/all_to_all | solution.py:227
  50.5 0.0 copy-done
  50.5 0.0 copy-done.1
  50.5 1.5 %finish.1 = f32[2048,128]{1,0:T(8,128)} custom-call(bf16[2048,128]{1,0:T(8,128)(2,1)S(1)} %bitcast.11, bf16[2048,128]{1,0:T(8,128)(2,1)S(1)} %get-tuple-element.12.normed_ref, f32[1,128]{1,0:T(1,128)S(1)} %get-tuple-element.13.gain_ref, f32[1,128]{1,0:T(1,128)S(1)} %get-tuple-element.14.bias_ref, bf16[128,128]{1,0:T(8,128)(2,1)S(1)} %copy-done, ...), custom_call_target="tpu_custom_call" | custom-call | tf_op jit(solution)/shard_map/finish/pallas_call | solution.py:230
Async XLA Ops:
  32.7 17.7 %copy-start = (bf16[128,128]{1,0:T(8,128)(2,1)S(1)}, bf16[128,128]{1,0:T(8,128)(2,1)}, u32[]{:S(2)}) copy-start(bf16[128,128]{1,0:T(8,128)(2,1)} %wg_ref.1) | copy-start | bytes 98308
  32.7 17.7 %copy-start.1 = (bf16[128,128]{1,0:T(8,128)(2,1)S(1)}, bf16[128,128]{1,0:T(8,128)(2,1)}, u32[]{:S(2)}) copy-start(bf16[128,128]{1,0:T(8,128)(2,1)} %w_ref.1) | copy-start | bytes 98308

commit v6 on v5

--- a/solution.py
+++ b/solution.py
@@ -149,18 +149,17 @@
         )
         update = jax.nn.sigmoid(gate) * projected
         for member in range(4):
-            low, high = pair_positions(first + member)
+            rows = pl.ds((first + member) * COLS, COLS)
             middle = member * 128 + COLS
-            out_ref[pl.ds(low, COLS), :] = update[middle - COLS : middle]
-            out_ref[pl.ds(high, COLS), :] = update[middle : middle + COLS]
-        if first + 4 in (8, SLABS):
-            begin = 0 if first + 4 == 8 else 8
-            for start in pair_positions(begin):
-                rows = pl.ds(start, (first + 4 - begin) * COLS)
-                copies.append(
-                    pltpu.make_async_copy(out_ref.at[rows], out_hbm.at[rows], sem.at[len(copies)])
-                )
-                copies[-1].start()
+            out_ref[0, rows, :] = update[middle - COLS : middle]
+            out_ref[1, rows, :] = update[middle : middle + COLS]
+        if first + 4 in (4, 8, 12, 16):
+            begin = first + 4 - 4
+            rows = pl.ds(begin * COLS, 4 * COLS)
+            copies.append(
+                pltpu.make_async_copy(out_ref.at[:, rows], out_hbm.at[:, rows], sem.at[len(copies)])
+            )
+            copies[-1].start()
     for copy in copies:
         copy.wait()
 
@@ -229,11 +228,11 @@
     )
     update = pl.pallas_call(
         finish_kernel,
-        out_shape=jax.ShapeDtypeStruct((POSITIONS, CH), jnp.float32),
+        out_shape=jax.ShapeDtypeStruct((2, POSITIONS // 2, CH), jnp.float32),
         out_specs=pl.BlockSpec(memory_space=pltpu.HBM),
         scratch_shapes=[
             pltpu.VMEM(((CH + 2) * OUT_PITCH, 128), jnp.float32),
-            pltpu.VMEM((POSITIONS, CH), jnp.float32),
+            pltpu.VMEM((2, POSITIONS // 2, CH), jnp.float32),
             pltpu.SemaphoreType.DMA((4,)),
         ],
         compiler_params=params,

time: 52.2 us -> 52.2 us (level)
  no operation moved by 1% of the time
where the time goes in v6:
time: 52.2 us; the launch traced here: 51.9 us
  blocking collectives  47.4 us (91%)
  Pallas kernels  4.47 us (9%)
    all_to_all x1, blocking collectives, per_device(): lax.all_to_all(sent.reshape(devices, 2 * SLABS, 128), ('row', 'col'), 0,...  29.7 us
    all_to_all x1, blocking collectives, per_device(): lax.all_to_all(mixed.reshape(devices, SLABS, 128), ('row', 'col'), 0, 0,...  17.7 us
    pallas_call x1, Pallas kernels, per_device(): pl.pallas_call(project_kernel, out_shape=(jax.ShapeDtypeStruct((CH * 2 *...  2.25 us
    pallas_call x1, Pallas kernels, per_device(): pl.pallas_call(finish_kernel, out_shape=jax.ShapeDtypeStruct((2, POSITION...  1.47 us

profile of v6, /device:TPU:1, one launch (start us, length us, event | category | flops | bytes accessed | tf_op | source)
XLA Modules:
  0.0 51.9 jit_solution(3094334830946275669)
XLA Ops:
  0.0 2.3 %project.1 = (bf16[4096,128]{1,0:T(8,128)(2,1)S(1)}, bf16[2048,128]{1,0:T(8,128)(2,1)S(1)}) custom-call(bf16[2048,128]{1,0:T(8,128)(2,1)} %bitcast.14, f32[1,128]{1,0:T(1,128)} %bitcast.17, f32[1,128]{1,0:T(1,128)} %bitcast.18, bf16[128,128]{1,0:T(8,128)(2,1)} %wlg_hbm.1, bf16[128,128]{1,0:T(8,128)(2,1)} %wl_hbm.1, bf16[128,128]{1,0:T(8,128)(2,1)} %wrg_hbm.1, ...), custom_call_target="tpu_custom_call" | custom-call | tf_op jit(solution)/shard_map/project/pallas_call | solution.py:185
  2.3 29.7 %all_to_all.10 = bf16[128,32,128]{2,1,0:T(8,128)(2,1)S(1)} all-to-all(bf16[128,32,128]{2,1,0:T(8,128)(2,1)S(1)} %bitcast.12), channel_id=1, replica_groups=mesh['row'=16,'col'=8] {'row','col'}, dimensions={0} | all-to-all | bytes 2097152 | tf_op jit(solution)/shard_map/all_to_all | solution.py:202
  32.0 0.7 %mix.1 = (bf16[2048,128]{1,0:T(8,128)(2,1)S(1)}, f32[1,128]{1,0:T(1,128)S(1)}, f32[1,128]{1,0:T(1,128)S(1)}) custom-call(bf16[4096,128]{1,0:T(8,128)(2,1)S(1)} %bitcast.10, f32[1,128]{1,0:T(1,128)} %bitcast.15, f32[1,128]{1,0:T(1,128)} %bitcast.16), custom_call_target="tpu_custom_call" | custom-call | tf_op jit(solution)/shard_map/mix/pallas_call | solution.py:206
  32.7 0.0 copy-start
  32.7 0.0 copy-start.1
  32.8 17.7 %all_to_all.11 = bf16[128,16,128]{2,1,0:T(8,128)(2,1)S(1)} all-to-all(bf16[128,16,128]{2,1,0:T(8,128)(2,1)S(1)} %bitcast.13), channel_id=1, replica_groups=mesh['row'=16,'col'=8] {'row','col'}, dimensions={0} | all-to-all | bytes 1048576 | tf_op jit(solution)/shard_map/all_to_all | solution.py:226
  50.5 0.0 copy-done
  50.5 0.0 copy-done.1
  50.5 1.5 %finish.1 = f32[2,1024,128]{2,1,0:T(8,128)} custom-call(bf16[2048,128]{1,0:T(8,128)(2,1)S(1)} %bitcast.11, bf16[2048,128]{1,0:T(8,128)(2,1)S(1)} %get-tuple-element.12.normed_ref, f32[1,128]{1,0:T(1,128)S(1)} %get-tuple-element.13.gain_ref, f32[1,128]{1,0:T(1,128)S(1)} %get-tuple-element.14.bias_ref, bf16[128,128]{1,0:T(8,128)(2,1)S(1)} %copy-done, ...), custom_call_target="tpu_custom_call" | custom-call | tf_op jit(solution)/shard_map/finish/pallas_call | solution.py:229
Async XLA Ops:
  32.7 17.7 %copy-start = (bf16[128,128]{1,0:T(8,128)(2,1)S(1)}, bf16[128,128]{1,0:T(8,128)(2,1)}, u32[]{:S(2)}) copy-start(bf16[128,128]{1,0:T(8,128)(2,1)} %wg_ref.1) | copy-start | bytes 98308
  32.7 17.7 %copy-start.1 = (bf16[128,128]{1,0:T(8,128)(2,1)S(1)}, bf16[128,128]{1,0:T(8,128)(2,1)}, u32[]{:S(2)}) copy-start(bf16[128,128]{1,0:T(8,128)(2,1)} %w_ref.1) | copy-start | bytes 98308

commit v7 on v6

--- a/solution.py
+++ b/solution.py
@@ -49,18 +49,18 @@
     weights = jnp.concatenate([jnp.transpose(kept[k]) for k in range(4)], 0)
     gain, bias = norm[0:1, :], norm[1:2, :]
     copy_x.wait()
-    for pair in range(SLABS // 2):
+    for pair in range(SLABS // 4):
         normed = jnp.concatenate(
-            [input_norm(x, gain, bias, 2 * pair + member) for member in range(2)], 0
-        )
-        normed_ref[pl.ds(pair * 256, 256), :] = normed
+            [input_norm(x, gain, bias, 4 * pair + member) for member in range(4)], 0
+        )
+        normed_ref[pl.ds(pair * 512, 512), :] = normed
         both = lax.dot_general(
             weights, normed, (((1,), (1,)), ((), ())), preferred_element_type=jnp.float32
         )
         left = jax.nn.sigmoid(both[:CH]) * both[CH : 2 * CH]
         right = jax.nn.sigmoid(both[2 * CH : 3 * CH]) * both[3 * CH :]
-        for member in range(2):
-            slab = 2 * pair + member
+        for member in range(4):
+            slab = 4 * pair + member
             lanes = slice(member * 128, member * 128 + 128)
             wide[pl.ds(slab, CH, stride=PITCH), :] = left[:, lanes]
             wide[pl.ds(SLABS + slab, CH, stride=PITCH), :] = right[:, lanes]
@@ -99,7 +99,7 @@
             right[...],
             (((1,), (1,)), ((), ())),
             preferred_element_type=jnp.float32,
-        )
+        ).astype(jnp.bfloat16)
         for inner in range(8):
             for m in range(n_col // 2):
                 lanes = slice(m * 128, m * 128 + 128)
@@ -107,9 +107,7 @@
                 bottom = block[inner * ROWS + HALF : (inner + 1) * ROWS, lanes]
                 for half in range(2):
                     start = ((r + inner) * n_col + 2 * m + half) * SLABS
-                    out_ref[pl.ds(start, SLABS), :] = side_by_side(top, bottom, half).astype(
-                        jnp.bfloat16
-                    )
+                    out_ref[pl.ds(start, SLABS), :] = side_by_side(top, bottom, half)
     for copy in copies:
         copy.wait()
 

time: 52.2 us -> 52.2 us (level)
  no operation moved by 1% of the time
where the time goes in v7:
time: 52.2 us; the launch traced here: 51.9 us
  blocking collectives  47.4 us (91%)
  Pallas kernels  4.46 us (9%)
    all_to_all x1, blocking collectives, per_device(): lax.all_to_all(sent.reshape(devices, 2 * SLABS, 128), ('row', 'col'), 0,...  29.7 us
    all_to_all x1, blocking collectives, per_device(): lax.all_to_all(mixed.reshape(devices, SLABS, 128), ('row', 'col'), 0, 0,...  17.7 us
    pallas_call x1, Pallas kernels, per_device(): pl.pallas_call(project_kernel, out_shape=(jax.ShapeDtypeStruct((CH * 2 *...  2.25 us
    pallas_call x1, Pallas kernels, per_device(): pl.pallas_call(finish_kernel, out_shape=jax.ShapeDtypeStruct((2, POSITION...  1.47 us

profile of v7, /device:TPU:1, one launch (start us, length us, event | category | flops | bytes accessed | tf_op | source)
XLA Modules:
  0.0 51.9 jit_solution(7563891366992751966)
XLA Ops:
  0.0 2.3 %project.1 = (bf16[4096,128]{1,0:T(8,128)(2,1)S(1)}, bf16[2048,128]{1,0:T(8,128)(2,1)S(1)}) custom-call(bf16[2048,128]{1,0:T(8,128)(2,1)} %bitcast.14, f32[1,128]{1,0:T(1,128)} %bitcast.17, f32[1,128]{1,0:T(1,128)} %bitcast.18, bf16[128,128]{1,0:T(8,128)(2,1)} %wlg_hbm.1, bf16[128,128]{1,0:T(8,128)(2,1)} %wl_hbm.1, bf16[128,128]{1,0:T(8,128)(2,1)} %wrg_hbm.1, ...), custom_call_target="tpu_custom_call" | custom-call | tf_op jit(solution)/shard_map/project/pallas_call | solution.py:183
  2.3 29.7 %all_to_all.10 = bf16[128,32,128]{2,1,0:T(8,128)(2,1)S(1)} all-to-all(bf16[128,32,128]{2,1,0:T(8,128)(2,1)S(1)} %bitcast.12), channel_id=1, replica_groups=mesh['row'=16,'col'=8] {'row','col'}, dimensions={0} | all-to-all | bytes 2097152 | tf_op jit(solution)/shard_map/all_to_all | solution.py:200
  32.0 0.7 %mix.1 = (bf16[2048,128]{1,0:T(8,128)(2,1)S(1)}, f32[1,128]{1,0:T(1,128)S(1)}, f32[1,128]{1,0:T(1,128)S(1)}) custom-call(bf16[4096,128]{1,0:T(8,128)(2,1)S(1)} %bitcast.10, f32[1,128]{1,0:T(1,128)} %bitcast.15, f32[1,128]{1,0:T(1,128)} %bitcast.16), custom_call_target="tpu_custom_call" | custom-call | tf_op jit(solution)/shard_map/mix/pallas_call | solution.py:204
  32.7 0.0 copy-start
  32.7 0.0 copy-start.1
  32.8 17.7 %all_to_all.11 = bf16[128,16,128]{2,1,0:T(8,128)(2,1)S(1)} all-to-all(bf16[128,16,128]{2,1,0:T(8,128)(2,1)S(1)} %bitcast.13), channel_id=1, replica_groups=mesh['row'=16,'col'=8] {'row','col'}, dimensions={0} | all-to-all | bytes 1048576 | tf_op jit(solution)/shard_map/all_to_all | solution.py:224
  50.5 0.0 copy-done
  50.5 0.0 copy-done.1
  50.5 1.5 %finish.1 = f32[2,1024,128]{2,1,0:T(8,128)} custom-call(bf16[2048,128]{1,0:T(8,128)(2,1)S(1)} %bitcast.11, bf16[2048,128]{1,0:T(8,128)(2,1)S(1)} %get-tuple-element.12.normed_ref, f32[1,128]{1,0:T(1,128)S(1)} %get-tuple-element.13.gain_ref, f32[1,128]{1,0:T(1,128)S(1)} %get-tuple-element.14.bias_ref, bf16[128,128]{1,0:T(8,128)(2,1)S(1)} %copy-done, ...), custom_call_target="tpu_custom_call" | custom-call | tf_op jit(solution)/shard_map/finish/pallas_call | solution.py:227
Async XLA Ops:
  32.7 17.7 %copy-start = (bf16[128,128]{1,0:T(8,128)(2,1)S(1)}, bf16[128,128]{1,0:T(8,128)(2,1)}, u32[]{:S(2)}) copy-start(bf16[128,128]{1,0:T(8,128)(2,1)} %wg_ref.1) | copy-start | bytes 98308
  32.7 17.7 %copy-start.1 = (bf16[128,128]{1,0:T(8,128)(2,1)S(1)}, bf16[128,128]{1,0:T(8,128)(2,1)}, u32[]{:S(2)}) copy-start(bf16[128,128]{1,0:T(8,128)(2,1)} %w_ref.1) | copy-start | bytes 98308
